TPU v7x, 128 devices: a whole 4x4x4 slice. The times are simulated.
128 devices in a mesh: node: 32 (over z, y, core), rep: 4 (over x).
Axes of the slice: x: 4, y: 4, z: 4, core: 2. Of those that a mesh axis runs over, the one named last changes fastest.
Arguments:
- memory: bfloat16 [131072, 256], P('node'), may hold values from -6 to 6
- req_rows: int32 [128, 32, 256], P(('node', 'rep')), may hold values from 0 to 4095, as said below
- src_slot: int32 [131072], P(('node', 'rep')), may hold values from 0 to 7967, as said below
- dst_slot: int32 [131072], P(('node', 'rep')), may hold values from 0 to 8191
- nbr_slot: int32 [131072, 10], P(('node', 'rep')), may hold values from 0 to 8191
- event_time: int32 [131072], P(('node', 'rep')), may hold values from 2000 to 2999
- nbr_time: int32 [131072, 10], P(('node', 'rep')), may hold values from 1000 to 2998, as said below
- frequency: float32 [128], replicated, may hold values from 0.001 to 0.1
- emb_grad: bfloat16 [131072, 256], P(('node', 'rep')), may hold values from -0.03125 to 0.03125
- w_input: bfloat16 [256, 768], replicated, may hold values from -0.375 to 0.375
- w_hidden: bfloat16 [256, 768], replicated, may hold values from -0.375 to 0.375
- w_time: bfloat16 [128, 256], replicated, may hold values from -0.5 to 0.5
- w_query: bfloat16 [256, 256], replicated, may hold values from -0.375 to 0.375
- w_key: bfloat16 [256, 256], replicated, may hold values from -0.375 to 0.375
- w_value: bfloat16 [256, 256], replicated, may hold values from -0.375 to 0.375
- w_out: bfloat16 [256, 256], replicated, may hold values from -0.375 to 0.375
Outputs:
- new_memory: bfloat16 [131072, 256], P('node')
- grad_input: float32 [256, 768], replicated
- grad_hidden: float32 [256, 768], replicated
- grad_time: float32 [128, 256], replicated
- grad_query: float32 [256, 256], replicated
- grad_key: float32 [256, 256], replicated
- grad_value: float32 [256, 256], replicated
- grad_out: float32 [256, 256], replicated
Inputs may be any that keep to these rules, and one draw needn't show every extreme that they name: `req_rows`: for each device and owner, 256 distinct rows of that owner's 4096 rows. `src_slot`: the position s % 256 is below 32, so a device's updated rows lie in the leading 32 slots of each owner's list. `nbr_time`: each lies 1 to 1000 below its event's time.
All inputs are finite; a program needn't handle non-finite values.
Results may differ from a plain program's by a relative error of at most 0.014.
Values may be sent and summed in bfloat16 or wider, within the bound.
No kernel may reach another device: no remote copies, remote signals or barrier semaphores. Data moves between devices by JAX's collectives and lax.ppermute only.
A program may use at most 128 MiB of HBM per device.

v0:
```python
import math

import jax
import jax.numpy as jnp
from jax import lax
from jax.sharding import PartitionSpec as P

HEADS = 8
UCAP = 32


def event_forward(weights, frequency, mem_src, mem_dst, mem_nbr, spacing, nudges):
    w_input, w_hidden, w_time, w_query, w_key, w_value, w_out = weights
    row_count, row_width = mem_src.shape
    neighbours = mem_nbr.shape[1]
    head_size = row_width // HEADS
    gate_in = jnp.dot(mem_dst, w_input, preferred_element_type=jnp.float32) + nudges[0]
    gate_hid = jnp.dot(mem_src, w_hidden, preferred_element_type=jnp.float32) + nudges[1]
    reset_gate = jax.nn.sigmoid(gate_in[:, :row_width] + gate_hid[:, :row_width])
    update = jax.nn.sigmoid(
        gate_in[:, row_width : 2 * row_width] + gate_hid[:, row_width : 2 * row_width]
    )
    candidate = jnp.tanh(gate_in[:, 2 * row_width :] + reset_gate * gate_hid[:, 2 * row_width :])
    hidden = (1.0 - update) * candidate + update * mem_src.astype(jnp.float32)
    hidden_half = hidden.astype(jnp.bfloat16)
    query = (jnp.dot(hidden_half, w_query, preferred_element_type=jnp.float32) + nudges[2]).astype(
        jnp.bfloat16
    )
    phase_rows = (
        jnp.cos(spacing[:, :, None] * frequency)
        .astype(jnp.bfloat16)
        .reshape(row_count * neighbours, -1)
    )
    mixed_rows = mem_nbr.reshape(row_count * neighbours, row_width).astype(jnp.float32)
    mixed_rows = (
        mixed_rows + jnp.dot(phase_rows, w_time, preferred_element_type=jnp.float32) + nudges[3]
    )
    mixed_rows = mixed_rows.astype(jnp.bfloat16)
    key_rows = (jnp.dot(mixed_rows, w_key, preferred_element_type=jnp.float32) + nudges[4]).astype(
        jnp.bfloat16
    )
    value_rows = (
        jnp.dot(mixed_rows, w_value, preferred_element_type=jnp.float32) + nudges[5]
    ).astype(jnp.bfloat16)
    key_rows = key_rows.reshape(row_count, neighbours, HEADS, head_size)
    value_rows = value_rows.reshape(row_count, neighbours, HEADS, head_size)
    query_heads = query.reshape(row_count, HEADS, head_size)
    scores = jnp.einsum(
        "ehd,ekhd->ehk", query_heads.astype(jnp.float32), key_rows.astype(jnp.float32)
    ) * head_size ** (-0.5)
    exponent = jnp.exp(scores)
    attention = (exponent / jnp.sum(exponent, axis=2, keepdims=True)).astype(jnp.bfloat16)
    attended = jnp.einsum(
        "ehk,ekhd->ehd", attention.astype(jnp.float32), value_rows.astype(jnp.float32)
    )
    attended = attended.astype(jnp.bfloat16).reshape(row_count, row_width)
    embedding = jnp.dot(attended, w_out, preferred_element_type=jnp.float32) + nudges[6] + hidden
    return (embedding, (hidden, hidden_half, phase_rows, mixed_rows, attended))


def outer_sum(left_rows, slope):
    return lax.dot_general(
        left_rows,
        slope.astype(jnp.bfloat16),
        (((0,), (0,)), ((), ())),
        preferred_element_type=jnp.float32,
    )


def event_grads(weights, frequency, mem_src, mem_dst, mem_nbr, spacing, slope_in):
    row_count, row_width = mem_src.shape
    flat_rows = row_count * mem_nbr.shape[1]
    nudges = (
        jnp.zeros((row_count, 3 * row_width), jnp.float32),
        jnp.zeros((row_count, 3 * row_width), jnp.float32),
        jnp.zeros((row_count, row_width), jnp.float32),
        jnp.zeros((flat_rows, row_width), jnp.float32),
        jnp.zeros((flat_rows, row_width), jnp.float32),
        jnp.zeros((flat_rows, row_width), jnp.float32),
        jnp.zeros((row_count, row_width), jnp.float32),
    )

    def forward(shifts):
        return event_forward(weights, frequency, mem_src, mem_dst, mem_nbr, spacing, shifts)

    embedding, pullback, saved_terms = jax.vjp(forward, nudges, has_aux=True)
    slopes = pullback(slope_in.astype(jnp.float32))[0]
    hidden, hidden_half, phase_rows, mixed_rows, attended = saved_terms
    weight_grads = (
        outer_sum(mem_dst, slopes[0]),
        outer_sum(mem_src, slopes[1]),
        outer_sum(phase_rows, slopes[3]),
        outer_sum(hidden_half, slopes[2]),
        outer_sum(mixed_rows, slopes[4]),
        outer_sum(mixed_rows, slopes[5]),
        outer_sum(attended, slopes[6]),
    )
    return (weight_grads, hidden)


def local(
    memory,
    req_rows,
    src_slot,
    dst_slot,
    nbr_slot,
    event_time,
    nbr_time,
    frequency,
    emb_grad,
    w_input,
    w_hidden,
    w_time,
    w_query,
    w_key,
    w_value,
    w_out,
):
    weights = (w_input, w_hidden, w_time, w_query, w_key, w_value, w_out)
    requests = req_rows[0]
    owners, capacity = requests.shape
    row_width = memory.shape[1]
    asked_rows = lax.all_to_all(requests, "node", split_axis=0, concat_axis=0, tiled=True)
    served = jnp.take(memory, asked_rows.reshape(-1), axis=0).reshape(owners, capacity, row_width)
    fetched = lax.all_to_all(served, "node", split_axis=0, concat_axis=0, tiled=True).reshape(
        owners * capacity, row_width
    )
    events = src_slot.shape[0]
    neighbours = nbr_slot.shape[1]
    block_rows = math.gcd(events, 512)
    block_count = events // block_rows
    spacing_all = (event_time[:, None] - nbr_time).astype(jnp.float32)
    blocks = (
        src_slot.reshape(block_count, block_rows),
        dst_slot.reshape(block_count, block_rows),
        nbr_slot.reshape(block_count, block_rows, neighbours),
        spacing_all.reshape(block_count, block_rows, neighbours),
        emb_grad.reshape(block_count, block_rows, row_width),
    )

    def one_block(state_pair, block_data):
        totals, slot_change = state_pair
        source, target, neighbour, spacing, slope_in = block_data
        mem_src = jnp.take(fetched, source, axis=0)
        mem_dst = jnp.take(fetched, target, axis=0)
        mem_nbr = jnp.take(fetched, neighbour, axis=0)
        weight_grads, hidden = event_grads(
            weights, frequency, mem_src, mem_dst, mem_nbr, spacing, slope_in
        )
        totals = jax.tree.map(jnp.add, totals, weight_grads)
        update_slot = source // capacity * UCAP + source % capacity
        slot_change = slot_change.at[update_slot].add(hidden - mem_src.astype(jnp.float32))
        return ((totals, slot_change), None)

    start = (
        jax.tree.map(lambda weight: jnp.zeros(weight.shape, jnp.float32), weights),
        jnp.zeros((owners * UCAP, row_width), jnp.float32),
    )
    (totals, slot_change), _ = lax.scan(one_block, start, blocks)
    summed = lax.psum(totals, ("node", "rep"))
    returned = lax.all_to_all(
        slot_change.reshape(owners, UCAP, row_width),
        "node",
        split_axis=0,
        concat_axis=0,
        tiled=True,
    )
    updated_rows = asked_rows[:, :UCAP]
    blank = jnp.zeros(memory.shape, jnp.float32)
    change = blank.at[updated_rows.reshape(-1)].add(returned.reshape(-1, row_width))
    change = lax.psum(change, "rep")
    new_memory = (memory.astype(jnp.float32) + change).astype(jnp.bfloat16)
    return (new_memory, summed[0], summed[1], summed[2], summed[3], summed[4], summed[5], summed[6])


def solution(mesh):
    placed = (
        P("node", None),
        P(("node", "rep"), None, None),
        P(("node", "rep")),
        P(("node", "rep")),
        P(("node", "rep"), None),
        P(("node", "rep")),
        P(("node", "rep"), None),
        P(),
        P(("node", "rep"), None),
        P(),
        P(),
        P(),
        P(),
        P(),
        P(),
        P(),
    )
    return jax.shard_map(
        local,
        mesh=mesh,
        in_specs=placed,
        out_specs=(P("node", None), P(), P(), P(), P(), P(), P(), P()),
        check_vma=False,
    )
```

profile of v0, /device:TPU:1, one launch (start us, length us, event | category | flops | bytes accessed | tf_op | source)
XLA Modules:
  0.0 884.2 jit_solution(1218876702535681784)
XLA Ops:
  8.0 16.7 %all_to_all.22 = s32[32,1,256]{2,1,0:T(1,128)S(1)} all-to-all(s32[32,1,256]{2,1,0:T(1,128)S(1)} %all_to_all.14), channel_id=1, replica_groups=mesh['node'=32,'rep'=4] {'node'}, dimensions={0} | all-to-all | bytes 65536 | tf_op jit(solution)/shard_map/all_to_all | solution.py:123
  24.7 33.0 %gather_fusion.3 = bf16[8192,256]{1,0:T(8,128)(2,1)} fusion(bf16[4096,256]{1,0:T(8,128)(2,1)} %param.20, s32[8192]{0:T(1024)S(1)} %broadcast_clamp_fusion.1), kind=kCustom, calls=%fused_computation.3 | custom fusion | bytes 8421376 | tf_op jit(solution)/shard_map/jit(_take)/gather | solution.py:124
  70.7 47.6 %all-to-all-done.1 = bf16[32,256,256]{2,1,0:T(8,128)(2,1)} async-done(((bf16[32,256,256]{2,1,0:T(8,128)(2,1)}), bf16[32,256,256]{2,1,0:T(8,128)(2,1)}, u32[]{:S(2)}, u32[]{:S(2)}) %all-to-all-start.1) | async-done | bytes 4194336 | tf_op jit(solution)/shard_map/all_to_all | solution.py:125
  119.3 465.2 %while.27 = (s32[]{:T(128)}, f32[256,768]{1,0:T(8,128)}, f32[256,768]{1,0:T(8,128)}, f32[128,256]{1,0:T(8,128)}, f32[256,256]{1,0:T(8,128)}, /*index=5*/f32[256,...) while((s32[]{:T(128)}, f32[256,768]{1,0:T(8,128)}, ...), condition=%wide.region_4.6_spmd.clone, body=%wide.region_0.5_spmd.clone.sunk | while | flops 5886112768 | bytes 215215200 | solution.py:159
  159.3 22.5 %gather_fusion.2 = bf16[5120,256]{1,0:T(8,128)(2,1)} fusion(bf16[8192,256]{1,0:T(8,128)(2,1)} %get-tuple-element.688, s32[5120]{0:T(1024)S(1)} %broadcast_clamp_fusion.3), kind=kCustom, calls=%fused_computation.2.clone.clone.1 | custom fusion | bytes 5263360 | tf_op jit(solution)/shard_map/while/body/eval_jaxpr/jit(_take)/gather | solution.py:146
  183.2 13.5 %fusion.160 = bf16[5120,256]{1,0:T(8,128)(2,1)S(1)} fusion(bf16[128,256]{1,0:T(8,128)(2,1)} %get-tuple-element.697, bf16[5120,256]{1,0:T(8,128)(2,1)} %gather_fusion.2, pred[5120]{0:T(1024)(128)(4,1)S(1)} %compare_and_fusion.7, f32[128]{0:T(128)} %get-tuple-element.696, f32[5120]{0:T(1024)S(1)} %mul.344), kind=kOutput, calls=%fused_computation.15.clone.1 | convolution fusion | flops 342097920 | bytes 5334528 | tf_op jit(solution)/shard_map/while/body/eval_jaxpr/jvp()/dot_general | solution.py:36
  199.0 12.1 %reshape.486 = bf16[512,10,8,32]{3,2,1,0:T(8,128)(2,1)} reshape(bf16[5120,256]{1,0:T(8,128)(2,1)} %convolution_convert_fusion.13) | data formatting | bytes 5242880 | tf_op jit(solution)/shard_map/while/body/eval_jaxpr/jvp()/reshape | solution.py:45
  211.1 9.4 %multiply_reduce_fusion.7 = f32[512,8,10]{1,2,0:T(8,128)S(1)} fusion(f32[512,8,32]{2,1,0:T(8,128)} %copy.75, bf16[512,10,8,32]{3,2,1,0:T(8,128)(2,1)} %reshape.486), kind=kLoop, calls=%fused_computation.8.clone.1 | loop fusion | flops 3891200 | bytes 3309568 | tf_op jit(solution)/shard_map/while/body/eval_jaxpr/jvp(ehd,ekhd->ehk)/dot_general | solution.py:48
  229.7 12.1 %reshape.487 = bf16[512,10,8,32]{3,2,1,0:T(8,128)(2,1)} reshape(bf16[5120,256]{1,0:T(8,128)(2,1)} %convolution_convert_fusion.15) | data formatting | bytes 5242880 | tf_op jit(solution)/shard_map/while/body/eval_jaxpr/jvp()/reshape | solution.py:46
  241.7 9.3 %multiply_reduce_fusion.8 = bf16[512,8,10]{1,2,0:T(8,128)(2,1)S(1)} fusion(f32[512,8,32]{2,1,0:T(8,128)} %copy.76, bf16[512,10,8,32]{3,2,1,0:T(8,128)(2,1)} %reshape.487), kind=kLoop, calls=%fused_computation.9.clone.1 | loop fusion | flops 3891200 | bytes 3227648 | tf_op jit(solution)/shard_map/while/body/eval_jaxpr/transpose(jvp(ehk,ekhd->ehd))/dot_general | solution.py:53
  258.4 10.3 %fusion.164 = (bf16[512,10,8,32]{3,2,1,0:T(8,128)(2,1)}, bf16[512,8,32]{2,1,0:T(8,128)(2,1)}) fusion(f32[512,8,10]{1,2,0:T(8,128)S(1)} %get-tuple-element.618, f32[512,8,32]{2,1,0:T(8,128)S(1)} %copy-done.6, bf16[512,10,8,32]{3,2,1,0:T(8,128)(2,1)S(1)} %bitcast.174), kind=kLoop, calls=%fused_computation.13.clone.1 | loop fusion | flops 6422528 | bytes 6193152 | tf_op jit(solution)/shard_map/while/body/eval_jaxpr/transpose(jvp())/convert_element_type | solution.py:49
  280.6 13.3 %reshape.488 = bf16[5120,256]{1,0:T(8,128)(2,1)} reshape(bf16[512,10,8,32]{3,2,1,0:T(8,128)(2,1)} %get-tuple-element.623) | data formatting | bytes 5242880 | tf_op jit(solution)/shard_map/while/body/eval_jaxpr/transpose(jvp())/reshape | solution.py:45
  298.1 8.1 fusion.167
  306.2 13.3 %reshape.489 = bf16[5120,256]{1,0:T(8,128)(2,1)} reshape(bf16[512,10,8,32]{3,2,1,0:T(8,128)(2,1)} %fusion.167) | data formatting | bytes 5242880 | tf_op jit(solution)/shard_map/while/body/eval_jaxpr/transpose(jvp())/reshape | solution.py:46
  319.5 11.1 %cosine_convert_fusion.12 = bf16[5120,128]{1,0:T(8,128)(2,1)} fusion(f32[128]{0:T(128)} %get-tuple-element.696, f32[5120]{0:T(1024)} %copy-done.23), kind=kLoop, calls=%fused_computation.31.clone.clone.clone.clone.2.clone.1 | loop fusion | flops 1310720 | bytes 1331712 | tf_op jit(solution)/shard_map/while/body/eval_jaxpr/dot_general | solution.py:62
  342.5 10.8 %multiply_reduce_fusion.9 = bf16[512,8,32]{2,1,0:T(8,128)(2,1)S(1)} fusion(f32[512,8,10]{1,2,0:T(8,128)S(1)} %copy-done.3, bf16[512,10,8,32]{3,2,1,0:T(8,128)(2,1)} %reshape.487), kind=kLoop, calls=%fused_computation.6.clone.1 | loop fusion | flops 3801088 | bytes 3047424 | tf_op jit(solution)/shard_map/while
  378.6 22.5 %gather_fusion.2 = bf16[5120,256]{1,0:T(8,128)(2,1)} fusion(bf16[8192,256]{1,0:T(8,128)(2,1)} %get-tuple-element.688, s32[5120]{0:T(1024)S(1)} %broadcast_clamp_fusion.3), kind=kCustom, calls=%fused_computation.2.clone.clone.1 | custom fusion | bytes 5263360 | tf_op jit(solution)/shard_map/while/body/eval_jaxpr/jit(_take)/gather | solution.py:146
  402.4 13.5 %fusion.160 = bf16[5120,256]{1,0:T(8,128)(2,1)S(1)} fusion(bf16[128,256]{1,0:T(8,128)(2,1)} %get-tuple-element.697, bf16[5120,256]{1,0:T(8,128)(2,1)} %gather_fusion.2, pred[5120]{0:T(1024)(128)(4,1)S(1)} %compare_and_fusion.7, f32[128]{0:T(128)} %get-tuple-element.696, f32[5120]{0:T(1024)S(1)} %mul.344), kind=kOutput, calls=%fused_computation.15.clone.1 | convolution fusion | flops 342097920 | bytes 5334528 | tf_op jit(solution)/shard_map/while/body/eval_jaxpr/jvp()/dot_general | solution.py:36
  418.3 12.1 %reshape.486 = bf16[512,10,8,32]{3,2,1,0:T(8,128)(2,1)} reshape(bf16[5120,256]{1,0:T(8,128)(2,1)} %convolution_convert_fusion.13) | data formatting | bytes 5242880 | tf_op jit(solution)/shard_map/while/body/eval_jaxpr/jvp()/reshape | solution.py:45
  430.3 9.4 %multiply_reduce_fusion.7 = f32[512,8,10]{1,2,0:T(8,128)S(1)} fusion(f32[512,8,32]{2,1,0:T(8,128)} %copy.75, bf16[512,10,8,32]{3,2,1,0:T(8,128)(2,1)} %reshape.486), kind=kLoop, calls=%fused_computation.8.clone.1 | loop fusion | flops 3891200 | bytes 3309568 | tf_op jit(solution)/shard_map/while/body/eval_jaxpr/jvp(ehd,ekhd->ehk)/dot_general | solution.py:48
  448.9 12.1 %reshape.487 = bf16[512,10,8,32]{3,2,1,0:T(8,128)(2,1)} reshape(bf16[5120,256]{1,0:T(8,128)(2,1)} %convolution_convert_fusion.15) | data formatting | bytes 5242880 | tf_op jit(solution)/shard_map/while/body/eval_jaxpr/jvp()/reshape | solution.py:46
  461.0 9.3 %multiply_reduce_fusion.8 = bf16[512,8,10]{1,2,0:T(8,128)(2,1)S(1)} fusion(f32[512,8,32]{2,1,0:T(8,128)} %copy.76, bf16[512,10,8,32]{3,2,1,0:T(8,128)(2,1)} %reshape.487), kind=kLoop, calls=%fused_computation.9.clone.1 | loop fusion | flops 3891200 | bytes 3227648 | tf_op jit(solution)/shard_map/while/body/eval_jaxpr/transpose(jvp(ehk,ekhd->ehd))/dot_general | solution.py:53
  477.6 10.3 %fusion.164 = (bf16[512,10,8,32]{3,2,1,0:T(8,128)(2,1)}, bf16[512,8,32]{2,1,0:T(8,128)(2,1)}) fusion(f32[512,8,10]{1,2,0:T(8,128)S(1)} %get-tuple-element.618, f32[512,8,32]{2,1,0:T(8,128)S(1)} %copy-done.6, bf16[512,10,8,32]{3,2,1,0:T(8,128)(2,1)S(1)} %bitcast.174), kind=kLoop, calls=%fused_computation.13.clone.1 | loop fusion | flops 6422528 | bytes 6193152 | tf_op jit(solution)/shard_map/while/body/eval_jaxpr/transpose(jvp())/convert_element_type | solution.py:49
  500.1 13.3 %reshape.488 = bf16[5120,256]{1,0:T(8,128)(2,1)} reshape(bf16[512,10,8,32]{3,2,1,0:T(8,128)(2,1)} %get-tuple-element.623) | data formatting | bytes 5242880 | tf_op jit(solution)/shard_map/while/body/eval_jaxpr/transpose(jvp())/reshape | solution.py:45
  517.6 8.1 fusion.167
  525.7 13.3 %reshape.489 = bf16[5120,256]{1,0:T(8,128)(2,1)} reshape(bf16[512,10,8,32]{3,2,1,0:T(8,128)(2,1)} %fusion.167) | data formatting | bytes 5242880 | tf_op jit(solution)/shard_map/while/body/eval_jaxpr/transpose(jvp())/reshape | solution.py:46
  539.0 11.1 %cosine_convert_fusion.12 = bf16[5120,128]{1,0:T(8,128)(2,1)} fusion(f32[128]{0:T(128)} %get-tuple-element.696, f32[5120]{0:T(1024)} %copy-done.23), kind=kLoop, calls=%fused_computation.31.clone.clone.clone.clone.2.clone.1 | loop fusion | flops 1310720 | bytes 1331712 | tf_op jit(solution)/shard_map/while/body/eval_jaxpr/dot_general | solution.py:62
  563.3 10.8 %multiply_reduce_fusion.9 = bf16[512,8,32]{2,1,0:T(8,128)(2,1)S(1)} fusion(f32[512,8,10]{1,2,0:T(8,128)S(1)} %copy-done.3, bf16[512,10,8,32]{3,2,1,0:T(8,128)(2,1)} %reshape.487), kind=kLoop, calls=%fused_computation.6.clone.1 | loop fusion | flops 3801088 | bytes 3047424 | tf_op jit(solution)/shard_map/while
  592.5 16.4 %all-to-all-done.2 = f32[32,32,256]{2,1,0:T(8,128)S(1)} async-done(((f32[32,32,256]{2,1,0:T(8,128)}), f32[32,32,256]{2,1,0:T(8,128)S(1)}, u32[]{:S(2)}, u32[]{:S(2)}) %all-to-all-start.2) | async-done | bytes 1048608 | tf_op jit(solution)/shard_map/all_to_all | solution.py:161
  608.9 8.3 scatter_custom_fusion.1
  617.9 89.5 %all-reduce.8.cloned.1.call-done = f32[4096,256]{1,0:T(8,128)} async-done(((f32[4096,256]{1,0:T(8,128)}), f32[4096,256]{1,0:T(8,128)}) %all-reduce.8.cloned.1.call-update) | async-done | bytes 4194320 | tf_op jit(solution)/shard_map/psum | solution.py:171
  711.4 158.1 %all-reduce.10.cloned.1.call-done = (f32[256,768]{1,0:T(8,128)}, f32[256,768]{1,0:T(8,128)}, f32[128,256]{1,0:T(8,128)}, f32[256,256]{1,0:T(8,128)}, f32[256,256...) async-done(((f32[256,768]{1,0:T(8,128)}, f32[256,768]{1,0:T(8,128)}, f32[128,256]{1,0:T(8,128)}, f32[256,256]{1,0:T(8,128)}, f32[256,256]{1,0:T(8,128)}, ...) | async-done | bytes 2752528 | tf_op jit(solution)/shard_map/psum | solution.py:160
  (264 shorter events, 183.0 us)
Async XLA Ops:
  24.6 33.0 %copy-start.26 = (s32[32,1,256]{2,1,0:T(1,128)}, s32[32,1,256]{2,1,0:T(1,128)S(1)}, u32[]{:S(2)}) copy-start(s32[32,1,256]{2,1,0:T(1,128)S(1)} %all_to_all.22) | copy-start | bytes 98308
  62.9 5.1 copy-start.35
  62.9 5.1 copy-start.36
  62.9 5.7 copy-start.32
  62.9 6.8 copy-start.33
  62.9 6.8 copy-start.34
  62.9 56.4 %copy-start.15 = (bf16[256,256]{1,0:T(8,128)(2,1)S(1)}, bf16[256,256]{1,0:T(8,128)(2,1)}, u32[]{:S(2)}) copy-start(bf16[256,256]{1,0:T(8,128)(2,1)} %param.33) | copy-start | bytes 393220
  62.9 55.4 %all-to-all-start.1 = ((bf16[32,256,256]{2,1,0:T(8,128)(2,1)}), bf16[32,256,256]{2,1,0:T(8,128)(2,1)}, u32[]{:S(2)}, u32[]{:S(2)}) async-start(bf16[32,256,256]{2,1,0:T(8,128)(2,1)} %broadcast_select_fusion.7), calls=%async_computation.1 | async-start | bytes 8388608 | tf_op jit(solution)/shard_map/all_to_all | solution.py:125
  147.2 7.9 copy-start.7
  183.1 13.5 %copy-start.23 = (f32[5120]{0:T(1024)}, f32[5120]{0:T(1024)S(1)}, u32[]{:S(2)}) copy-start(f32[5120]{0:T(1024)S(1)} %mul.344) | copy-start | bytes 61444 | tf_op jit(solution)/shard_map/while
  241.7 9.4 %copy-start.1 = (f32[512,8,10]{1,2,0:T(8,128)S(1)}, f32[512,8,10]{1,2,0:T(8,128)}, u32[]{:S(2)}) copy-start(f32[512,8,10]{1,2,0:T(8,128)} %copy-done) | copy-start | bytes 491524 | tf_op jit(solution)/shard_map/while
  241.7 9.4 %copy-start.14 = (f32[512,8]{1,0:T(8,128)S(1)}, f32[512,8]{1,0:T(8,128)}, u32[]{:S(2)}) copy-start(f32[512,8]{1,0:T(8,128)} %multiply_divide_fusion.2) | copy-start | bytes 49156 | tf_op jit(solution)/shard_map/while
  252.8 5.6 copy-start.6
  342.5 11.6 %copy-start.19 = (bf16[2,512,256]{2,1,0:T(8,128)(2,1)S(1)}, bf16[2,512,256]{2,1,0:T(8,128)(2,1)}, u32[]{:S(2)}) copy-start(bf16[2,512,256]{2,1,0:T(8,128)(2,1)} %get-tuple-element.692) | copy-start | bytes 1572868 | tf_op jit(solution)/shard_map/while
  342.5 11.6 %copy-start.20 = (f32[256,256]{1,0:T(8,128)S(1)}, f32[256,256]{1,0:T(8,128)}, u32[]{:S(2)}) copy-start(f32[256,256]{1,0:T(8,128)} %get-tuple-element.659) | copy-start | bytes 786436 | tf_op jit(solution)/shard_map/while
  354.4 5.5 copy-start.21
  366.4 7.9 copy-start.7
  402.4 13.5 %copy-start.23 = (f32[5120]{0:T(1024)}, f32[5120]{0:T(1024)S(1)}, u32[]{:S(2)}) copy-start(f32[5120]{0:T(1024)S(1)} %mul.344) | copy-start | bytes 61444 | tf_op jit(solution)/shard_map/while
  461.0 9.4 %copy-start.1 = (f32[512,8,10]{1,2,0:T(8,128)S(1)}, f32[512,8,10]{1,2,0:T(8,128)}, u32[]{:S(2)}) copy-start(f32[512,8,10]{1,2,0:T(8,128)} %copy-done) | copy-start | bytes 491524 | tf_op jit(solution)/shard_map/while
  461.0 9.4 %copy-start.14 = (f32[512,8]{1,0:T(8,128)S(1)}, f32[512,8]{1,0:T(8,128)}, u32[]{:S(2)}) copy-start(f32[512,8]{1,0:T(8,128)} %multiply_divide_fusion.2) | copy-start | bytes 49156 | tf_op jit(solution)/shard_map/while
  472.1 5.0 slice-start.2
  472.1 5.6 copy-start.6
  563.3 11.6 %copy-start.19 = (bf16[2,512,256]{2,1,0:T(8,128)(2,1)S(1)}, bf16[2,512,256]{2,1,0:T(8,128)(2,1)}, u32[]{:S(2)}) copy-start(bf16[2,512,256]{2,1,0:T(8,128)(2,1)} %get-tuple-element.692) | copy-start | bytes 1572868 | tf_op jit(solution)/shard_map/while
  563.3 11.6 %copy-start.20 = (f32[256,256]{1,0:T(8,128)S(1)}, f32[256,256]{1,0:T(8,128)}, u32[]{:S(2)}) copy-start(f32[256,256]{1,0:T(8,128)} %get-tuple-element.659) | copy-start | bytes 786436 | tf_op jit(solution)/shard_map/while
  575.2 5.5 copy-start.21
  584.5 24.4 %all-to-all-start.2 = ((f32[32,32,256]{2,1,0:T(8,128)}), f32[32,32,256]{2,1,0:T(8,128)S(1)}, u32[]{:S(2)}, u32[]{:S(2)}) async-start(f32[32,32,256]{2,1,0:T(8,128)} %bitcast.182), calls=%async_computation.2 | async-start | bytes 2097152 | tf_op jit(solution)/shard_map/all_to_all | solution.py:161
  591.6 115.8 %all-reduce.8.cloned.1.call-start = ((), (), s32[]{:S(2)}) async-start(), calls=%async_computation.3 | async-start | bytes 8388608 | tf_op jit(solution)/shard_map/psum | solution.py:171
  617.2 90.3 %copy-start.4 = (bf16[4096,256]{1,0:T(8,128)(2,1)S(1)}, bf16[4096,256]{1,0:T(8,128)(2,1)}, u32[]{:S(2)}) copy-start(bf16[4096,256]{1,0:T(8,128)(2,1)} %param.20) | copy-start | bytes 6291460
  617.2 252.3 %all-reduce.10.cloned.1.call-start = ((), (), s32[]{:S(2)}) async-start(), calls=%async_computation.4 | async-start | bytes 5505024 | tf_op jit(solution)/shard_map/psum | solution.py:160
  869.5 5.6 copy-start.29
  869.5 6.3 copy-start.28
  869.5 7.0 copy-start.27
  (43 other events, 127.1 us)
Sparse Core Ops, SparseCore 0:
  617.3 90.0 all-reduce.7
  715.0 154.4 all-reduce.9
where the time goes:
time: 892 us; the launch traced here: 884 us
  waiting for transfers between devices  312 us (35%)
  local copies, waits for them, and re-layouts  237 us (27%)
  other arithmetic  170 us (19%)
  matrix products  95.8 us (11%)
  loops' own time  25.9 us (3%)
  blocking collectives  16.7 us (2%)
  between operations  14.4 us (2%)
  starting transfers between devices  12.1 us (1%)
    psum x1, waiting for transfers between devices, local(): summed = lax.psum(totals, ('node', 'rep'))  158 us
    psum x1, waiting for transfers between devices, local(): change = lax.psum(change, 'rep')  89.5 us
    reshape x4, local copies, waits for them, and re-layouts, event_forward(): key_rows = key_rows.reshape(row_count, neighbours, HEADS, head_size)  50.7 us
    reshape x4, local copies, waits for them, and re-layouts, event_forward(): value_rows = value_rows.reshape(row_count, neighbours, HEADS, head_size)  50.7 us
    all_to_all x1, waiting for transfers between devices, local(): lax.all_to_all(served, 'node', split_axis=0, concat_axis=0, tiled=True)  47.6 us
    gather x2, local copies, waits for them, and re-layouts, one_block(): mem_nbr = jnp.take(fetched, neighbour, axis=0)  45 us
    gather x1, local copies, waits for them, and re-layouts, local(): jnp.take(memory, asked_rows.reshape(-1), axis=0)  33 us
    dot_general x14, matrix products, outer_sum(): lax.dot_general(left_rows, slope.astype(jnp.bfloat16), (((0,), (0,)), (()...  32.6 us
  transfers between devices with their start and end apart: 4, of which 4 were waited for; matrix products, arithmetic and copies ran while one was open for 1% of the time, Pallas kernels for 0%

commit v1 on v0

v1 whole, which is shorter than its diff:
```python
import math

import jax
import jax.numpy as jnp
from jax import lax
from jax.experimental import pallas as pl
from jax.experimental.pallas import tpu as pltpu
from jax.sharding import PartitionSpec as P

HEADS = 8
UCAP = 32
F32 = jnp.float32
BF16 = jnp.bfloat16
VMEM = pl.BlockSpec(memory_space=pltpu.VMEM)
SMEM = pl.BlockSpec(memory_space=pltpu.SMEM)
LIMIT = 58 * 1024 * 1024


def dot(a, b):
    return jnp.dot(a, b, preferred_element_type=F32)


def dot_nt(a, b):
    return lax.dot_general(a, b, (((1,), (1,)), ((), ())), preferred_element_type=F32)


def dot_tn(a, b):
    return lax.dot_general(a, b, (((0,), (0,)), ((), ())), preferred_element_type=F32)


def spread_table(rows_ref, table, base, step):
    count = rows_ref.shape[0]

    def body(i, carry):
        block = rows_ref[pl.ds(pl.multiple_of(i * step, step), step), :].astype(F32)
        start = base + i * (2 * step)
        table[pl.ds(start, step, stride=2), :] = block[:, :128]
        table[pl.ds(start + 1, step, stride=2), :] = block[:, 128:]
        return carry

    lax.fori_loop(0, count // step, body, 0)


def pick_rows(index_ref, offset, table, stage, count):
    for r in range(count):
        row = index_ref[offset + r]
        stage[2 * r : 2 * r + 2, :] = table[pl.ds(2 * row, 2), :]


def joined(stage, start, count):
    left = stage[pl.ds(2 * start, count, stride=2), :]
    right = stage[pl.ds(2 * start + 1, count, stride=2), :]
    return jnp.concatenate([left, right], axis=1)


def serve_kernel(index_ref, rows_ref, out_ref, table, stage):
    spread_table(rows_ref, table, 0, 256)
    step = stage.shape[0] // 2

    def body(i, carry):
        base = pl.multiple_of(i * step, step)
        pick_rows(index_ref, base, table, stage, step)
        out_ref[pl.ds(base, step), :] = joined(stage, 0, step).astype(BF16)
        return carry

    lax.fori_loop(0, out_ref.shape[0] // step, body, 0)


def serve(index, memory):
    count = index.shape[0]
    rows, width = memory.shape
    return pl.pallas_call(
        serve_kernel,
        out_shape=jax.ShapeDtypeStruct((count, width), BF16),
        in_specs=[SMEM, VMEM],
        out_specs=VMEM,
        scratch_shapes=[pltpu.VMEM((2 * rows, 128), F32), pltpu.VMEM((256, 128), F32)],
        compiler_params=pltpu.CompilerParams(vmem_limit_bytes=LIMIT),
        name="serve_rows",
    )(index, memory)


def sigmoid(x):
    return 1.0 / (1.0 + jnp.exp(-x))


def gru_forward(mem_src, mem_dst, w_input_ref, w_hidden_ref):
    width = mem_src.shape[1]
    parts_in = [dot(mem_dst, w_input_ref[:, k * width : (k + 1) * width]) for k in range(3)]
    parts_hid = [dot(mem_src, w_hidden_ref[:, k * width : (k + 1) * width]) for k in range(3)]
    reset = sigmoid(parts_in[0] + parts_hid[0])
    update = sigmoid(parts_in[1] + parts_hid[1])
    candidate = jnp.tanh(parts_in[2] + reset * parts_hid[2])
    rows = mem_src.astype(F32)
    hidden = (1.0 - update) * candidate + update * rows
    return rows, reset, update, candidate, parts_hid[2], hidden


def memory_kernel(
    src_ref, dst_ref, src_row_ref, rows_ref, w_input_ref, w_hidden_ref,
    mem_src_ref, mem_dst_ref, change_ref, table, stage, delta,
):
    spread_table(rows_ref, table, 0, 256)
    step = stage.shape[0] // 4
    events = mem_src_ref.shape[0]

    def body(i, carry):
        base = pl.multiple_of(i * step, step)
        pick_rows(src_ref, base, table, stage, step)
        pick_rows(dst_ref, base, table, stage.at[pl.ds(2 * step, 2 * step)], step)
        mem_src = joined(stage, 0, step).astype(BF16)
        mem_dst = joined(stage, step, step).astype(BF16)
        mem_src_ref[pl.ds(base, step), :] = mem_src
        mem_dst_ref[pl.ds(base, step), :] = mem_dst
        rows, _, _, _, _, hidden = gru_forward(mem_src, mem_dst, w_input_ref, w_hidden_ref)
        delta[pl.ds(base, step), :] = (hidden - rows).astype(BF16)
        return carry

    lax.fori_loop(0, events // step, body, 0)
    source = src_row_ref[...]
    slot = (source >> 8) * UCAP + (source & 255)
    slots = change_ref.shape[0]
    part = 256
    for k in range(slots // part):
        ids = lax.broadcasted_iota(jnp.int32, (part, events), 0) + k * part
        picked = jnp.where(ids == slot, 1.0, 0.0).astype(BF16)
        change_ref[pl.ds(k * part, part), :] = dot(picked, delta[...]).astype(BF16)


def memory_step(src_slot, dst_slot, fetched, w_input, w_hidden):
    events = src_slot.shape[0]
    count, width = fetched.shape
    slots = count // 256 * UCAP
    return pl.pallas_call(
        memory_kernel,
        out_shape=(
            jax.ShapeDtypeStruct((events, width), BF16),
            jax.ShapeDtypeStruct((events, width), BF16),
            jax.ShapeDtypeStruct((slots, width), BF16),
        ),
        in_specs=[SMEM, SMEM, VMEM, VMEM, VMEM, VMEM],
        out_specs=(VMEM, VMEM, VMEM),
        scratch_shapes=[
            pltpu.VMEM((2 * count, 128), F32),
            pltpu.VMEM((512, 128), F32),
            pltpu.VMEM((events, width), BF16),
        ],
        compiler_params=pltpu.CompilerParams(vmem_limit_bytes=LIMIT),
        name="memory_step",
    )(src_slot, dst_slot, src_slot.reshape(1, events), fetched, w_input, w_hidden)


COS_TERMS = (
    1.0,
    -0.49999988079071045,
    0.041666485369205475,
    -0.001388777862302959,
    2.4769342417130247e-05,
    -2.7073761543761066e-07,
    1.7225967319234314e-09,
)
TURN_HIGH = 6.28125
TURN_LOW = 2.0 * math.pi - 6.28125


def cosine(x):
    turns = jnp.floor(x * (0.5 / math.pi) + 0.5)
    rest = (x - turns * TURN_HIGH) - turns * TURN_LOW
    square = rest * rest
    total = jnp.full_like(x, COS_TERMS[-1])
    for term in COS_TERMS[-2::-1]:
        total = total * square + term
    return total


def events_kernel(
    nbr_ref, rows_ref, spacing_ref, freq_ref, mem_src_ref, mem_dst_ref, slope_ref,
    w_input_ref, w_hidden_ref, w_time_ref, w_query_ref, w_key_ref, w_value_ref, w_out_ref,
    grads_ref,
    table, stage, ones, phase, mixed, keys, values, score, dprob, slopes, dmixed,
    acc_in, acc_hid, acc_time, acc_query, acc_kv, acc_out,
):
    nbrs = spacing_ref.shape[0]
    events, width = slope_ref.shape
    size = stage.shape[0] // (2 * nbrs)
    head = width // HEADS
    scale = head ** -0.5
    spread_table(rows_ref, table, 0, 256)
    row_id = lax.broadcasted_iota(jnp.int32, (width, width), 0) // head
    col_id = lax.broadcasted_iota(jnp.int32, (width, width), 1) // head
    ones[...] = jnp.where(row_id == col_id, 1.0, 0.0).astype(BF16)
    for acc in (acc_in, acc_hid, acc_time, acc_query, acc_kv, acc_out):
        acc[...] = jnp.zeros_like(acc)

    def body(b, carry):
        base = pl.multiple_of(b * size, size)

        def pick(i, c):
            first = i * 128
            j = first // size
            offset = j * events + base + (first - j * size)
            pick_rows(nbr_ref, offset, table, stage.at[pl.ds(pl.multiple_of(2 * first, 256), 256)], 128)
            return c

        lax.fori_loop(0, nbrs * size // 128, pick, 0)
        mem_src = mem_src_ref[pl.ds(base, size), :]
        mem_dst = mem_dst_ref[pl.ds(base, size), :]
        rows, reset, update, candidate, hid_c, hidden = gru_forward(
            mem_src, mem_dst, w_input_ref, w_hidden_ref
        )
        hidden_half = hidden.astype(BF16)
        query = dot(hidden_half, w_query_ref[...]).astype(BF16).astype(F32) * scale
        query_two = query * math.log2(math.e)
        for j in range(nbrs):
            span = pl.ds(j * size, size)
            angle = freq_ref[...] * spacing_ref[j : j + 1, pl.ds(base, size)]
            wave = cosine(angle).astype(BF16)
            phase[:, span] = wave
            mixed[span, :] = (joined(stage, j * size, size) + dot_tn(wave, w_time_ref[...])).astype(BF16)
        for j in range(nbrs):
            span = pl.ds(j * size, size)
            key = dot(mixed[span, :], w_key_ref[...])
            keys[span, :] = key.astype(BF16)
            values[span, :] = dot(mixed[span, :], w_value_ref[...]).astype(BF16)
            score[span, :] = dot((key * query_two).astype(BF16), ones[...])
        top = score[0:size, :]
        for j in range(1, nbrs):
            top = jnp.maximum(top, score[j * size : (j + 1) * size, :])
        total = jnp.zeros_like(top)
        for j in range(nbrs):
            span = pl.ds(j * size, size)
            weight = jnp.exp2(score[span, :] - top)
            score[span, :] = weight
            total = total + weight
        inverse = 1.0 / total
        slope = slope_ref[pl.ds(base, size), :]
        dattended = dot_nt(slope, w_out_ref[...]).astype(BF16).astype(F32)
        attended = jnp.zeros_like(top)
        overlap = jnp.zeros_like(top)
        for j in range(nbrs):
            span = pl.ds(j * size, size)
            prob = score[span, :] * inverse
            score[span, :] = prob
            prob_half = prob.astype(BF16).astype(F32)
            value = values[span, :].astype(F32)
            attended = attended + prob_half * value
            dvalue = (prob_half * dattended).astype(BF16)
            slopes[span, width:] = dvalue
            change = dot((dattended * value).astype(BF16), ones[...])
            dprob[span, :] = change
            overlap = overlap + prob * change
        attended_half = attended.astype(BF16)
        acc_out[...] += dot_tn(attended_half, slope)
        dquery = jnp.zeros_like(top)
        for j in range(nbrs):
            span = pl.ds(j * size, size)
            dscore = score[span, :] * (dprob[span, :] - overlap)
            dquery = dquery + dscore * keys[span, :].astype(F32)
            slopes[span, :width] = (dscore * query).astype(BF16)
        for j in range(nbrs):
            span = pl.ds(j * size, size)
            dmixed[span, :] = (
                dot_nt(slopes[span, :width], w_key_ref[...]) + dot_nt(slopes[span, width:], w_value_ref[...])
            ).astype(BF16)
        acc_kv[...] += dot_tn(mixed[...], slopes[...])
        acc_time[...] += dot(phase[...], dmixed[...])
        dquery_half = (dquery * scale).astype(BF16)
        acc_query[...] += dot_tn(hidden_half, dquery_half)
        dhidden = slope.astype(F32) + dot_nt(dquery_half, w_query_ref[...])
        dcand = dhidden * (1.0 - update) * (1.0 - candidate * candidate)
        dupdate = dhidden * (rows - candidate) * update * (1.0 - update)
        dreset = dcand * hid_c * reset * (1.0 - reset)
        dreset = dreset.astype(BF16)
        dupdate = dupdate.astype(BF16)
        for k, part in enumerate((dreset, dupdate, dcand.astype(BF16))):
            acc_in[:, k * width : (k + 1) * width] += dot_tn(mem_dst, part)
        for k, part in enumerate((dreset, dupdate, (dcand * reset).astype(BF16))):
            acc_hid[:, k * width : (k + 1) * width] += dot_tn(mem_src, part)
        return carry

    lax.fori_loop(0, events // size, body, 0)
    row = 0
    for acc in (acc_in, acc_hid, acc_time, acc_query, acc_kv, acc_out):
        depth, columns = acc.shape
        for k in range(columns // 128):
            grads_ref[row : row + depth, :] = acc[:, k * 128 : (k + 1) * 128].astype(BF16)
            row += depth
    if row < grads_ref.shape[0]:
        grads_ref[row:, :] = jnp.zeros((grads_ref.shape[0] - row, 128), BF16)


def events_step(nbr_index, fetched, spacing, frequency, mem_src, mem_dst, slope, weights, grad_rows, size=256):
    nbrs, events = spacing.shape
    count, width = fetched.shape
    freqs = frequency.shape[0]
    flat = nbrs * size
    return pl.pallas_call(
        events_kernel,
        out_shape=jax.ShapeDtypeStruct((grad_rows, 128), BF16),
        in_specs=[SMEM] + [VMEM] * 13,
        out_specs=VMEM,
        scratch_shapes=[
            pltpu.VMEM((2 * count, 128), F32),
            pltpu.VMEM((2 * flat, 128), F32),
            pltpu.VMEM((width, width), BF16),
            pltpu.VMEM((freqs, flat), BF16),
            pltpu.VMEM((flat, width), BF16),
            pltpu.VMEM((flat, width), BF16),
            pltpu.VMEM((flat, width), BF16),
            pltpu.VMEM((flat, width), F32),
            pltpu.VMEM((flat, width), F32),
            pltpu.VMEM((flat, 2 * width), BF16),
            pltpu.VMEM((flat, width), BF16),
            pltpu.VMEM((width, 3 * width), F32),
            pltpu.VMEM((width, 3 * width), F32),
            pltpu.VMEM((freqs, width), F32),
            pltpu.VMEM((width, width), F32),
            pltpu.VMEM((width, 2 * width), F32),
            pltpu.VMEM((width, width), F32),
        ],
        compiler_params=pltpu.CompilerParams(vmem_limit_bytes=LIMIT),
        name="events_step",
    )(nbr_index, fetched, spacing, frequency.reshape(freqs, 1), mem_src, mem_dst, slope, *weights)


def merge_kernel(index_ref, change_ref, memory_ref, out_ref, table, stage):
    rows = memory_ref.shape[0]
    spread_table(memory_ref, table, 0, 256)
    step = stage.shape[0] // 2
    group = 32

    def body(i, carry):
        base = pl.multiple_of(i * step, step)
        block = change_ref[pl.ds(base, step), :].astype(F32)
        stage[pl.ds(0, step, stride=2), :] = block[:, :128]
        stage[pl.ds(1, step, stride=2), :] = block[:, 128:]
        for g in range(step // group):
            spots = [pl.ds(2 * index_ref[base + g * group + r], 2) for r in range(group)]
            sums = [
                table[spots[r], :] + stage[2 * (g * group + r) : 2 * (g * group + r) + 2, :]
                for r in range(group)
            ]
            for r in range(group):
                table[spots[r], :] = sums[r]
        return carry

    lax.fori_loop(0, change_ref.shape[0] // step, body, 0)

    def finish(i, carry):
        base = pl.multiple_of(i * 256, 256)
        left = table[pl.ds(2 * base, 256, stride=2), :]
        right = table[pl.ds(2 * base + 1, 256, stride=2), :]
        out_ref[pl.ds(base, 256), :] = jnp.concatenate([left, right], axis=1).astype(BF16)
        return carry

    lax.fori_loop(0, rows // 256, finish, 0)


def merge(index, change, memory):
    rows, width = memory.shape
    return pl.pallas_call(
        merge_kernel,
        out_shape=jax.ShapeDtypeStruct((rows, width), BF16),
        in_specs=[SMEM, VMEM, VMEM],
        out_specs=VMEM,
        scratch_shapes=[pltpu.VMEM((2 * rows, 128), F32), pltpu.VMEM((256, 128), F32)],
        compiler_params=pltpu.CompilerParams(vmem_limit_bytes=LIMIT),
        name="merge_rows",
    )(index, change, memory)


def total_kernel(parts_ref, out_ref):
    total = jnp.zeros(parts_ref.shape[1:], F32)
    for k in range(parts_ref.shape[0]):
        total = total + parts_ref[k].astype(F32)
    total = total.astype(BF16)
    for k in range(parts_ref.shape[0]):
        out_ref[k] = total


def total_parts(parts):
    return pl.pallas_call(
        total_kernel,
        out_shape=jax.ShapeDtypeStruct(parts.shape, BF16),
        in_specs=[VMEM],
        out_specs=VMEM,
        compiler_params=pltpu.CompilerParams(vmem_limit_bytes=LIMIT),
        name="total_parts",
    )(parts)


def unpack_kernel(flat_ref, *out_refs):
    row = 0
    for out_ref in out_refs:
        depth, columns = out_ref.shape
        for k in range(columns // 128):
            out_ref[:, k * 128 : (k + 1) * 128] = flat_ref[row : row + depth, :].astype(F32)
            row += depth


def unpack(flat, shapes):
    return pl.pallas_call(
        unpack_kernel,
        out_shape=tuple(jax.ShapeDtypeStruct(shape, F32) for shape in shapes),
        in_specs=[VMEM],
        out_specs=tuple(VMEM for _ in shapes),
        compiler_params=pltpu.CompilerParams(vmem_limit_bytes=LIMIT),
        name="unpack_grads",
    )(flat)


BOTH = ("node", "rep")


def local(
    memory, req_rows, src_slot, dst_slot, nbr_slot, event_time, nbr_time, frequency, emb_grad,
    w_input, w_hidden, w_time, w_query, w_key, w_value, w_out,
):
    weights = (w_input, w_hidden, w_time, w_query, w_key, w_value, w_out)
    requests = req_rows[0]
    owners, capacity = requests.shape
    width = memory.shape[1]
    reps = lax.axis_size("rep")
    asked = lax.all_to_all(requests, "node", split_axis=0, concat_axis=0, tiled=True)
    served = serve(asked.reshape(-1), memory).reshape(owners, capacity, width)
    fetched = lax.all_to_all(served, "node", split_axis=0, concat_axis=0, tiled=True)
    fetched = fetched.reshape(owners * capacity, width)
    nbr_index = nbr_slot.T.reshape(-1)
    spacing = (event_time[None, :] - nbr_time.T).astype(F32)
    mem_src, mem_dst, change = memory_step(src_slot, dst_slot, fetched, w_input, w_hidden)
    spread = jnp.broadcast_to(
        change.reshape(owners, 1, UCAP, width), (owners, reps, UCAP, width)
    ).reshape(owners * reps * UCAP, width)
    updates = lax.all_to_all(spread, BOTH, split_axis=0, concat_axis=0, tiled=True)
    touched = lax.all_gather(asked[:, :UCAP], "rep")
    touched = jnp.transpose(touched, (1, 0, 2)).reshape(-1)
    shapes = (w_input.shape, w_hidden.shape, w_time.shape, w_query.shape, w_key.shape, w_value.shape, w_out.shape)
    used = sum(shape[0] * shape[1] for shape in shapes) // 128
    devices = owners * reps
    share = -(-used // (devices * 16)) * 16
    grads = events_step(nbr_index, fetched, spacing, frequency, mem_src, mem_dst, emb_grad, weights, devices * share)
    parts = lax.all_to_all(grads, BOTH, split_axis=0, concat_axis=0, tiled=True)
    summed = total_parts(parts.reshape(devices, share, 128))
    flat = lax.all_to_all(summed.reshape(devices * share, 128), BOTH, split_axis=0, concat_axis=0, tiled=True)
    new_memory = merge(touched, updates, memory)
    return (new_memory, *unpack(flat, shapes))


def solution(mesh):
    split = P(BOTH)
    placed = (
        P("node", None), P(BOTH, None, None), split, split, P(BOTH, None), split, P(BOTH, None),
        P(), P(BOTH, None), P(), P(), P(), P(), P(), P(), P(),
    )
    return jax.shard_map(
        local,
        mesh=mesh,
        in_specs=placed,
        out_specs=(P("node", None), P(), P(), P(), P(), P(), P(), P()),
        check_vma=False,
    )
```

time: 892 us -> 254 us (0.28)
  waiting for transfers between devices: 312 us -> 76.4 us
  local copies, waits for them, and re-layouts: 237 us -> 4.53 us
  other arithmetic: 170 us -> 0.64 us
  matrix products: 95.8 us -> 0 us
  Pallas kernels: 0 us -> 82.3 us
  blocking collectives: 16.7 us -> 74.3 us
  loops' own time: 25.9 us -> 0 us
  between operations: 14.4 us -> 0.71 us
    psum x2 -> x0, waiting for transfers between devices: 248 us -> none  [the longest x1 158 us: local(): summed = lax.psum(totals, ('node', 'rep'))]
    reshape x11 -> x3, local copies, waits for them, and re-layouts: 102 us -> 2.07 us  [the longest x1 0.74 us: events_step(): frequency.reshape(freqs, 1)]
    gather x7 -> x0, local copies, waits for them, and re-layouts: 96.2 us -> none  [the longest x2 45 us: one_block(): mem_nbr = jnp.take(fetched, neighbour, axis=0)]
    dot_general x32 -> x0, matrix products: 95.8 us -> none  [the longest x14 32.6 us: outer_sum(): lax.dot_general(left_rows, slope.astype(jnp.bfloat16), (((0,), (0,)), (()...]
    pallas_call x0 -> x6, Pallas kernels: none -> 82.3 us  [the longest x1 43.9 us: events_step(): pl.pallas_call(events_kernel, out_shape=jax.ShapeDtypeStruct((grad_rows,...]
    dot_general x6 -> x0, other arithmetic: 59.6 us -> none  [the longest x2 22.2 us: outer_sum(): lax.dot_general(left_rows, slope.astype(jnp.bfloat16), (((0,), (0,)), (()...]
    convert_element_type x8 -> x1, other arithmetic: 43.7 us -> 0.64 us  [local(): spacing = (event_time[None, :] - nbr_time.T).astype(F32)]
    all_to_all x0 -> x1, blocking collectives: none -> 33.3 us  [local(): parts = lax.all_to_all(grads, BOTH, split_axis=0, concat_axis=0, tiled=True)]
  transfers between devices with their start and end apart: 4 -> 3, of which waited for: 4 -> 2; matrix products, arithmetic and copies ran while one was open for 1% -> 1% of each run, Pallas kernels for 0% -> 5%
where the time goes in v1:
time: 254 us; the launch traced here: 253 us
  Pallas kernels  82.3 us (32%)
  waiting for transfers between devices  76.4 us (30%)
  blocking collectives  74.3 us (29%)
  starting transfers between devices  13.7 us (5%)
  local copies, waits for them, and re-layouts  4.53 us (2%)
    all_to_all x1, waiting for transfers between devices, local(): lax.all_to_all(served, 'node', split_axis=0, concat_axis=0, tiled=True)  48.4 us
    pallas_call x1, Pallas kernels, events_step(): pl.pallas_call(events_kernel, out_shape=jax.ShapeDtypeStruct((grad_rows,...  43.9 us
    all_to_all x1, blocking collectives, local(): parts = lax.all_to_all(grads, BOTH, split_axis=0, concat_axis=0, tiled=True)  33.3 us
    all_to_all x1, waiting for transfers between devices, local(): lax.all_to_all(spread, BOTH, split_axis=0, concat_axis=0, tiled=True)  28.1 us
    all_gather x1, blocking collectives, local(): touched = lax.all_gather(asked[:, :UCAP], 'rep')  24.2 us
    all_to_all x1, blocking collectives, local(): lax.all_to_all(requests, 'node', split_axis=0, concat_axis=0, tiled=True)  16.8 us
    pallas_call x1, Pallas kernels, serve(): pl.pallas_call(serve_kernel, out_shape=jax.ShapeDtypeStruct((count, width...  13.1 us
    pallas_call x1, Pallas kernels, merge(): pl.pallas_call(merge_kernel, out_shape=jax.ShapeDtypeStruct((rows, width)...  11 us
  transfers between devices with their start and end apart: 3, of which 2 were waited for; matrix products, arithmetic and copies ran while one was open for 1% of the time, Pallas kernels for 5%

profile of v1, /device:TPU:1, one launch (start us, length us, event | category | flops | bytes accessed | tf_op | source)
XLA Modules:
  0.0 252.6 jit_solution(37168726926938534)
XLA Ops:
  0.6 0.8 all_to_all.29
  1.4 16.8 %all_to_all.45 = s32[32,1,256]{2,1,0:T(1,128)} all-to-all(s32[32,1,256]{2,1,0:T(1,128)S(1)} %all_to_all.29), channel_id=1, replica_groups=mesh['node'=32,'rep'=4] {'node'}, dimensions={0} | all-to-all | bytes 65536 | tf_op jit(solution)/shard_map/all_to_all | solution.py:424
  18.2 13.1 %serve_rows.1 = bf16[8192,256]{1,0:T(8,128)(2,1)} custom-call(s32[8192]{0:T(1024)} %bitcast.25, bf16[4096,256]{1,0:T(8,128)(2,1)} %memory_ref.1), custom_call_target="tpu_custom_call" | custom-call | tf_op jit(solution)/shard_map/serve_rows/pallas_call | solution.py:72
  31.2 0.0 copy-start.6
  31.2 0.0 copy-start.4
  31.2 0.0 copy-start.3
  31.2 0.0 copy-start.5
  31.2 5.0 %all-to-all-start.1 = ((bf16[32,256,256]{2,1,0:T(8,128)(2,1)}), bf16[32,256,256]{2,1,0:T(8,128)(2,1)}, u32[]{:S(2)}, u32[]{:S(2)}) async-start(bf16[32,256,256]{2,1,0:T(8,128)(2,1)} %bitcast.20), calls=%async_computation.1 | async-start | bytes 8388608 | tf_op jit(solution)/shard_map/all_to_all | solution.py:426
  36.2 0.0 copy-done.6
  36.2 0.7 copy.28.freq_ref
  37.0 0.0 copy-done.4
  37.0 0.6 reshape.61.nbr_ref
  37.6 0.0 copy-done.3
  37.6 0.0 copy-done.5
  37.6 0.6 convert_bitcast_fusion.spacing_ref
  38.3 48.4 %all-to-all-done.1 = bf16[32,256,256]{2,1,0:T(8,128)(2,1)} async-done(((bf16[32,256,256]{2,1,0:T(8,128)(2,1)}), bf16[32,256,256]{2,1,0:T(8,128)(2,1)}, u32[]{:S(2)}, u32[]{:S(2)}) %all-to-all-start.1) | async-done | bytes 4194336 | tf_op jit(solution)/shard_map/all_to_all | solution.py:426
  86.6 8.5 %memory_step.1 = (bf16[1024,256]{1,0:T(8,128)(2,1)}, bf16[1024,256]{1,0:T(8,128)(2,1)}, bf16[1024,256]{1,0:T(8,128)(2,1)}) custom-call(s32[1024]{0:T(1024)} %src_ref.1, s32[1024]{0:T(1024)} %dst_ref.1, s32[1,1024]{1,0:T(1,128)} %bitcast.30, bf16[8192,256]{1,0:T(8,128)(2,1)} %bitcast.5.rows_ref, bf16[256,768]{1,0:T(8,128)(2,1)} %w_input_ref.3, ...), custom_call_target="tpu_custom_call" | custom-call | tf_op jit(solution)/shard_map/memory_step/pallas_call | solution.py:134
  95.1 43.9 %events_step.1 = bf16[6144,128]{1,0:T(8,128)(2,1)} custom-call(s32[10240]{0:T(1024)} %reshape.61.nbr_ref, bf16[8192,256]{1,0:T(8,128)(2,1)} %bitcast.5.rows_ref, f32[10,1024]{1,0:T(8,128)} %convert_bitcast_fusion.spacing_ref, f32[128,1]{1,0:T(8,128)} %copy.28.freq_ref, bf16[1024,256]{1,0:T(8,128)(2,1)} %get-tuple-element.19.mem_src_ref, ...), custom_call_target="tpu_custom_call" | custom-call | tf_op jit(solution)/shard_map/events_step/pallas_call | solution.py:297
  139.0 33.3 %all_to_all.46.parts_ref = bf16[128,48,128]{2,1,0:T(8,128)(2,1)} all-to-all(bf16[128,48,128]{2,1,0:T(8,128)(2,1)} %bitcast.23), channel_id=1, replica_groups=mesh['node'=32,'rep'=4] {'node','rep'}, dimensions={0} | all-to-all | bytes 3145728 | tf_op jit(solution)/shard_map/all_to_all | solution.py:442
  172.3 0.0 copy-done.1
  172.3 1.6 broadcast_in_dim.9
  173.9 3.8 %all-to-all-start.2 = ((bf16[128,32,256]{2,1,0:T(8,128)(2,1)}), bf16[128,32,256]{2,1,0:T(8,128)(2,1)S(1)}, u32[]{:S(2)}, u32[]{:S(2)}) async-start(bf16[128,32,256]{2,1,0:T(8,128)(2,1)} %bitcast.22), calls=%async_computation.2 | async-start | bytes 4194304 | tf_op jit(solution)/shard_map/all_to_all | solution.py:434
  177.8 2.9 %total_parts.1 = bf16[128,48,128]{2,1,0:T(8,128)(2,1)} custom-call(bf16[128,48,128]{2,1,0:T(8,128)(2,1)} %all_to_all.46.parts_ref), custom_call_target="tpu_custom_call" | custom-call | tf_op jit(solution)/shard_map/total_parts/pallas_call | solution.py:382
  180.7 28.1 %all-to-all-done.2 = bf16[128,32,256]{2,1,0:T(8,128)(2,1)S(1)} async-done(((bf16[128,32,256]{2,1,0:T(8,128)(2,1)}), bf16[128,32,256]{2,1,0:T(8,128)(2,1)S(1)}, u32[]{:S(2)}, u32[]{:S(2)}) %all-to-all-start.2) | async-done | bytes 2097184 | tf_op jit(solution)/shard_map/all_to_all | solution.py:434
  208.8 4.9 %all-to-all-start.4 = ((bf16[128,48,128]{2,1,0:T(8,128)(2,1)}), bf16[128,48,128]{2,1,0:T(8,128)(2,1)}, u32[]{:S(2)}, u32[]{:S(2)}) async-start(bf16[128,48,128]{2,1,0:T(8,128)(2,1)} %total_parts.1), calls=%async_computation.4 | async-start | bytes 3145728 | tf_op jit(solution)/shard_map/all_to_all | solution.py:444
  213.6 0.0 copy-done.2
  213.7 24.2 %all-gather = s32[128,32]{1,0:T(8,128)S(1)} all-gather(s32[32,32]{1,0:T(8,128)S(1)} %slice.4), channel_id=2, replica_groups=mesh['node'=32,'rep'=4] {'rep'}, dimensions={0}, use_global_device_ids=true | all-gather | bytes 20480 | tf_op jit(solution)/shard_map/all_gather | solution.py:435
  237.9 0.7 reshape.56.index_ref
  238.6 0.0 copy-done
  238.6 11.0 %merge_rows.1 = bf16[4096,256]{1,0:T(8,128)(2,1)} custom-call(s32[4096]{0:T(1024)} %reshape.56.index_ref, bf16[4096,256]{1,0:T(8,128)(2,1)} %bitcast.21, bf16[4096,256]{1,0:T(8,128)(2,1)} %memory_ref.1), custom_call_target="tpu_custom_call" | custom-call | tf_op jit(solution)/shard_map/merge_rows/pallas_call | solution.py:361
  249.6 0.0 all-to-all-done.4
  249.6 3.0 %unpack_grads.1 = (f32[256,768]{1,0:T(8,128)}, f32[256,768]{1,0:T(8,128)}, f32[128,256]{1,0:T(8,128)}, f32[256,256]{1,0:T(8,128)}, f32[256,256]{1,0:T(8,128)}, /*index=5*/f32[256,256]{1,0:T(8,128)}, f32[256,256]{1,0:T(8,128)}) custom-call(bf16[6144,128]{1,0:T(8,128)(2,1)} %bitcast.13.flat_ref), custom_call_target="tpu_custom_call" | custom-call | tf_op jit(solution)/shard_map/unpack_grads/pallas_call | solution.py:402
  (6 shorter events, 0.1 us)
Async XLA Ops:
  31.2 5.0 %copy-start.6 = (f32[128]{0:T(128)S(1)}, f32[128]{0:T(128)}, u32[]{:S(2)}) copy-start(f32[128]{0:T(128)} %param.23) | copy-start | bytes 1540
  31.2 5.8 %copy-start.4 = (s32[1024,10]{0,1:T(8,128)S(1)}, s32[1024,10]{0,1:T(8,128)}, u32[]{:S(2)}) copy-start(s32[1024,10]{0,1:T(8,128)} %param.20) | copy-start | bytes 122884
  31.2 6.4 %copy-start.3 = (s32[1024,10]{0,1:T(8,128)S(1)}, s32[1024,10]{0,1:T(8,128)}, u32[]{:S(2)}) copy-start(s32[1024,10]{0,1:T(8,128)} %param.22) | copy-start | bytes 122884
  31.2 6.4 %copy-start.5 = (s32[1024]{0:T(1024)S(1)}, s32[1024]{0:T(1024)}, u32[]{:S(2)}) copy-start(s32[1024]{0:T(1024)} %param.21) | copy-start | bytes 12292
  31.2 55.4 %all-to-all-start.1 = ((bf16[32,256,256]{2,1,0:T(8,128)(2,1)}), bf16[32,256,256]{2,1,0:T(8,128)(2,1)}, u32[]{:S(2)}, u32[]{:S(2)}) async-start(bf16[32,256,256]{2,1,0:T(8,128)(2,1)} %bitcast.20), calls=%async_computation.1 | async-start | bytes 8388608 | tf_op jit(solution)/shard_map/all_to_all | solution.py:426
  139.0 33.3 %copy-start.1 = (bf16[1024,256]{1,0:T(8,128)(2,1)S(1)}, bf16[1024,256]{1,0:T(8,128)(2,1)}, u32[]{:S(2)}) copy-start(bf16[1024,256]{1,0:T(8,128)(2,1)} %get-tuple-element.18) | copy-start | bytes 1572868
  173.9 34.8 %all-to-all-start.2 = ((bf16[128,32,256]{2,1,0:T(8,128)(2,1)}), bf16[128,32,256]{2,1,0:T(8,128)(2,1)S(1)}, u32[]{:S(2)}, u32[]{:S(2)}) async-start(bf16[128,32,256]{2,1,0:T(8,128)(2,1)} %bitcast.22), calls=%async_computation.2 | async-start | bytes 4194304 | tf_op jit(solution)/shard_map/all_to_all | solution.py:434
  180.7 32.9 %copy-start.2 = (s32[32,1,256]{2,1,0:T(1,128)S(1)}, s32[32,1,256]{2,1,0:T(1,128)}, u32[]{:S(2)}) copy-start(s32[32,1,256]{2,1,0:T(1,128)} %all_to_all.45) | copy-start | bytes 98308
  208.8 29.9 %copy-start = (bf16[128,32,256]{2,1,0:T(8,128)(2,1)}, bf16[128,32,256]{2,1,0:T(8,128)(2,1)S(1)}, u32[]{:S(2)}) copy-start(bf16[128,32,256]{2,1,0:T(8,128)(2,1)S(1)} %all-to-all-done.2) | copy-start | bytes 6291460
  208.8 40.8 %all-to-all-start.4 = ((bf16[128,48,128]{2,1,0:T(8,128)(2,1)}), bf16[128,48,128]{2,1,0:T(8,128)(2,1)}, u32[]{:S(2)}, u32[]{:S(2)}) async-start(bf16[128,48,128]{2,1,0:T(8,128)(2,1)} %total_parts.1), calls=%async_computation.4 | async-start | bytes 3145728 | tf_op jit(solution)/shard_map/all_to_all | solution.py:444

commit v2 on v1

--- a/solution.py
+++ b/solution.py
@@ -16,6 +16,10 @@
 LIMIT = 58 * 1024 * 1024
 
 
+def cost(micros):
+    return pl.CostEstimate(flops=int(micros * 1.1e9), bytes_accessed=int(micros * 3.0e6), transcendentals=0)
+
+
 def dot(a, b):
     return jnp.dot(a, b, preferred_element_type=F32)
 
@@ -76,6 +80,7 @@
         out_specs=VMEM,
         scratch_shapes=[pltpu.VMEM((2 * rows, 128), F32), pltpu.VMEM((256, 128), F32)],
         compiler_params=pltpu.CompilerParams(vmem_limit_bytes=LIMIT),
+        cost_estimate=cost(13),
         name="serve_rows",
     )(index, memory)
 
@@ -146,6 +151,7 @@
             pltpu.VMEM((events, width), BF16),
         ],
         compiler_params=pltpu.CompilerParams(vmem_limit_bytes=LIMIT),
+        cost_estimate=cost(8),
         name="memory_step",
     )(src_slot, dst_slot, src_slot.reshape(1, events), fetched, w_input, w_hidden)
 
@@ -319,15 +325,19 @@
             pltpu.VMEM((width, width), F32),
         ],
         compiler_params=pltpu.CompilerParams(vmem_limit_bytes=LIMIT),
+        cost_estimate=cost(44),
         name="events_step",
     )(nbr_index, fetched, spacing, frequency.reshape(freqs, 1), mem_src, mem_dst, slope, *weights)
 
 
-def merge_kernel(index_ref, change_ref, memory_ref, out_ref, table, stage):
+def merge_kernel(place_ref, index_ref, change_ref, memory_ref, out_ref, table, stage):
     rows = memory_ref.shape[0]
     spread_table(memory_ref, table, 0, 256)
     step = stage.shape[0] // 2
-    group = 32
+    group = UCAP
+    reps = 4
+    owner_rows = change_ref.shape[0] // reps
+    here = place_ref[0]
 
     def body(i, carry):
         base = pl.multiple_of(i * step, step)
@@ -335,7 +345,9 @@
         stage[pl.ds(0, step, stride=2), :] = block[:, :128]
         stage[pl.ds(1, step, stride=2), :] = block[:, 128:]
         for g in range(step // group):
-            spots = [pl.ds(2 * index_ref[base + g * group + r], 2) for r in range(group)]
+            sender = i * (step // group) + g
+            first = lax.rem(here - lax.rem(sender, reps) + reps, reps) * owner_rows + sender // reps * group
+            spots = [pl.ds(2 * index_ref[first + r], 2) for r in range(group)]
             sums = [
                 table[spots[r], :] + stage[2 * (g * group + r) : 2 * (g * group + r) + 2, :]
                 for r in range(group)
@@ -356,17 +368,18 @@
     lax.fori_loop(0, rows // 256, finish, 0)
 
 
-def merge(index, change, memory):
+def merge(place, index, change, memory):
     rows, width = memory.shape
     return pl.pallas_call(
         merge_kernel,
         out_shape=jax.ShapeDtypeStruct((rows, width), BF16),
-        in_specs=[SMEM, VMEM, VMEM],
+        in_specs=[SMEM, SMEM, VMEM, VMEM],
         out_specs=VMEM,
         scratch_shapes=[pltpu.VMEM((2 * rows, 128), F32), pltpu.VMEM((256, 128), F32)],
         compiler_params=pltpu.CompilerParams(vmem_limit_bytes=LIMIT),
+        cost_estimate=cost(11),
         name="merge_rows",
-    )(index, change, memory)
+    )(place, index, change, memory)
 
 
 def total_kernel(parts_ref, out_ref):
@@ -385,6 +398,7 @@
         in_specs=[VMEM],
         out_specs=VMEM,
         compiler_params=pltpu.CompilerParams(vmem_limit_bytes=LIMIT),
+        cost_estimate=cost(3),
         name="total_parts",
     )(parts)
 
@@ -405,6 +419,7 @@
         in_specs=[VMEM],
         out_specs=tuple(VMEM for _ in shapes),
         compiler_params=pltpu.CompilerParams(vmem_limit_bytes=LIMIT),
+        cost_estimate=cost(3),
         name="unpack_grads",
     )(flat)
 
@@ -425,6 +440,13 @@
     served = serve(asked.reshape(-1), memory).reshape(owners, capacity, width)
     fetched = lax.all_to_all(served, "node", split_axis=0, concat_axis=0, tiled=True)
     fetched = fetched.reshape(owners * capacity, width)
+    lead = asked[:, :UCAP]
+    turned = [lead] + [
+        lax.ppermute(lead, "rep", [(i, (i + k) % reps) for i in range(reps)]) for k in range(1, reps)
+    ]
+    touched = jnp.stack(turned).reshape(-1)
+    place = lax.axis_index("rep").astype(jnp.int32).reshape(1)
+    fetched, touched = lax.optimization_barrier((fetched, touched))
     nbr_index = nbr_slot.T.reshape(-1)
     spacing = (event_time[None, :] - nbr_time.T).astype(F32)
     mem_src, mem_dst, change = memory_step(src_slot, dst_slot, fetched, w_input, w_hidden)
@@ -432,17 +454,16 @@
         change.reshape(owners, 1, UCAP, width), (owners, reps, UCAP, width)
     ).reshape(owners * reps * UCAP, width)
     updates = lax.all_to_all(spread, BOTH, split_axis=0, concat_axis=0, tiled=True)
-    touched = lax.all_gather(asked[:, :UCAP], "rep")
-    touched = jnp.transpose(touched, (1, 0, 2)).reshape(-1)
     shapes = (w_input.shape, w_hidden.shape, w_time.shape, w_query.shape, w_key.shape, w_value.shape, w_out.shape)
     used = sum(shape[0] * shape[1] for shape in shapes) // 128
     devices = owners * reps
     share = -(-used // (devices * 16)) * 16
     grads = events_step(nbr_index, fetched, spacing, frequency, mem_src, mem_dst, emb_grad, weights, devices * share)
+    grads, updates = lax.optimization_barrier((grads, updates))
     parts = lax.all_to_all(grads, BOTH, split_axis=0, concat_axis=0, tiled=True)
     summed = total_parts(parts.reshape(devices, share, 128))
     flat = lax.all_to_all(summed.reshape(devices * share, 128), BOTH, split_axis=0, concat_axis=0, tiled=True)
-    new_memory = merge(touched, updates, memory)
+    new_memory = merge(place, touched, updates, memory)
     return (new_memory, *unpack(flat, shapes))
 
 

time: 254 us -> 222 us (0.87)
  blocking collectives: 74.3 us -> 51.7 us
  waiting for transfers between devices: 76.4 us -> 56 us
  starting transfers between devices: 13.7 us -> 21.6 us
    all_to_all x1, waiting for transfers between devices: 28.1 us -> 0.01 us  [local(): lax.all_to_all(spread, BOTH, split_axis=0, concat_axis=0, tiled=True)]
    all_gather x1 -> x0, blocking collectives: 24.2 us -> none  [local(): touched = lax.all_gather(asked[:, :UCAP], 'rep')]
    all_to_all x1, waiting for transfers between devices: 0.01 us -> 13.2 us  [local(): lax.all_to_all(summed.reshape(devices * share, 128), BOTH, split_axis=0,...]
    all_to_all x1, waiting for transfers between devices: 48.4 us -> 42.7 us  [local(): lax.all_to_all(served, 'node', split_axis=0, concat_axis=0, tiled=True)]
    ppermute x0 -> x3, starting transfers between devices: none -> 4.88 us  [local(): lax.ppermute(lead, 'rep', [(i, (i + k) % reps) for i in range(reps)])]
    all_to_all x1, starting transfers between devices: 3.84 us -> 7.94 us  [local(): lax.all_to_all(spread, BOTH, split_axis=0, concat_axis=0, tiled=True)]
  transfers between devices with their start and end apart: 3 -> 6, of which waited for: 2 -> 2; matrix products, arithmetic and copies ran while one was open for 1% -> 1% of each run, Pallas kernels for 5% -> 25%
where the time goes in v2:
time: 222 us; the launch traced here: 221 us
  Pallas kernels  83.5 us (38%)
  waiting for transfers between devices  56 us (25%)
  blocking collectives  51.7 us (23%)
  starting transfers between devices  21.6 us (10%)
  local copies, waits for them, and re-layouts  6.67 us (3%)
    pallas_call x1, Pallas kernels, events_step(): pl.pallas_call(events_kernel, out_shape=jax.ShapeDtypeStruct((grad_rows,...  43.9 us
    all_to_all x1, waiting for transfers between devices, local(): lax.all_to_all(served, 'node', split_axis=0, concat_axis=0, tiled=True)  42.7 us
    all_to_all x1, blocking collectives, local(): parts = lax.all_to_all(grads, BOTH, split_axis=0, concat_axis=0, tiled=True)  35.1 us
    all_to_all x1, blocking collectives, local(): lax.all_to_all(requests, 'node', split_axis=0, concat_axis=0, tiled=True)  16.7 us
    all_to_all x1, waiting for transfers between devices, local(): lax.all_to_all(summed.reshape(devices * share, 128), BOTH, split_axis=0,...  13.2 us
    pallas_call x1, Pallas kernels, serve(): pl.pallas_call(serve_kernel, out_shape=jax.ShapeDtypeStruct((count, width...  13.1 us
    pallas_call x1, Pallas kernels, merge(): pl.pallas_call(merge_kernel, out_shape=jax.ShapeDtypeStruct((rows, width)...  12.1 us
    pallas_call x1, Pallas kernels, memory_step(): pl.pallas_call(memory_kernel, out_shape=(jax.ShapeDtypeStruct((events, wi...  8.47 us
  transfers between devices with their start and end apart: 6, of which 2 were waited for; matrix products, arithmetic and copies ran while one was open for 1% of the time, Pallas kernels for 25%

profile of v2, /device:TPU:1, one launch (start us, length us, event | category | flops | bytes accessed | tf_op | source)
XLA Modules:
  0.0 220.8 jit_solution(10096682606787113822)
XLA Ops:
  0.6 0.8 all_to_all.30
  1.4 16.7 %all_to_all.46 = s32[32,1,256]{2,1,0:T(1,128)} all-to-all(s32[32,1,256]{2,1,0:T(1,128)S(1)} %all_to_all.30), channel_id=1, replica_groups=mesh['node'=32,'rep'=4] {'node'}, dimensions={0} | all-to-all | bytes 65536 | tf_op jit(solution)/shard_map/all_to_all | solution.py:439
  18.1 13.1 %serve_rows.1 = bf16[8192,256]{1,0:T(8,128)(2,1)} custom-call(s32[8192]{0:T(1024)} %bitcast.27, bf16[4096,256]{1,0:T(8,128)(2,1)} %memory_ref.1), custom_call_target="tpu_custom_call" | custom-call | flops 14300000256 | bytes 39000000 | tf_op jit(solution)/shard_map/serve_rows/pallas_call | solution.py:76
  31.2 0.0 copy-start.4
  31.2 5.0 %all-to-all-start.1 = ((bf16[32,256,256]{2,1,0:T(8,128)(2,1)}), bf16[32,256,256]{2,1,0:T(8,128)(2,1)}, u32[]{:S(2)}, u32[]{:S(2)}) async-start(bf16[32,256,256]{2,1,0:T(8,128)(2,1)} %bitcast.22), calls=%async_computation.1 | async-start | bytes 8388608 | tf_op jit(solution)/shard_map/all_to_all | solution.py:441
  36.1 0.0 copy-done.2
  36.2 1.3 collective-permute-start
  37.4 2.5 %collective-permute-start.1 = (s32[32,32]{1,0:T(8,128)S(1)}, s32[32,32]{1,0:T(8,128)S(1)}, u32[]{:S(2)}, u32[]{:S(2)}) collective-permute-start(s32[32,32]{1,0:T(8,128)S(1)} %get-tuple-element.37), channel_id=1, source_target_pairs={{0,2},{1,3},{2,0},{3,1},{4,6},{5,7},{6,4},{7,5},{8,10},{9,11},{10,... | collective-permute-start | bytes 12296 | tf_op jit(solution)/shard_map/ppermute | solution.py:445
  39.9 1.2 collective-permute-start.2
  41.1 0.0 copy-done.3
  41.1 0.0 copy-done.5
  41.1 0.6 convert_bitcast_fusion.spacing_ref
  41.7 0.0 copy-done.6
  41.7 0.7 copy.25.freq_ref
  42.4 0.6 reshape.64.nbr_ref
  43.1 0.0 collective-permute-done
  43.1 0.0 collective-permute-done.1
  43.1 0.0 collective-permute-done.2
  43.1 0.7 reshape.63.index_ref
  43.8 42.7 %all-to-all-done.1 = bf16[32,256,256]{2,1,0:T(8,128)(2,1)} async-done(((bf16[32,256,256]{2,1,0:T(8,128)(2,1)}), bf16[32,256,256]{2,1,0:T(8,128)(2,1)}, u32[]{:S(2)}, u32[]{:S(2)}) %all-to-all-start.1) | async-done | bytes 4194336 | tf_op jit(solution)/shard_map/all_to_all | solution.py:441
  86.5 8.5 %memory_step.1 = (bf16[1024,256]{1,0:T(8,128)(2,1)}, bf16[1024,256]{1,0:T(8,128)(2,1)}, bf16[1024,256]{1,0:T(8,128)(2,1)}) custom-call(s32[1024]{0:T(1024)} %src_ref.1, s32[1024]{0:T(1024)} %dst_ref.1, s32[1,1024]{1,0:T(1,128)} %bitcast.34, bf16[8192,256]{1,0:T(8,128)(2,1)} %bitcast.3.rows_ref, bf16[256,768]{1,0:T(8,128)(2,1)} %w_input_ref.3, ...), custom_call_target="tpu_custom_call" | custom-call | flops 8800000000 | bytes 24000000 | tf_op jit(solution)/shard_map/memory_step/pallas_call | solution.py:139
  95.0 2.6 %broadcast_in_dim.9 = bf16[32,4,32,256]{3,2,1,0:T(8,128)(2,1)} broadcast(bf16[32,32,256]{2,1,0:T(8,128)(2,1)} %bitcast.26), dimensions={0,2,3} | broadcast | bytes 2621440 | tf_op jit(solution)/shard_map/broadcast_in_dim | solution.py:453
  97.6 7.9 %all-to-all-start.2 = ((bf16[128,32,256]{2,1,0:T(8,128)(2,1)}), bf16[128,32,256]{2,1,0:T(8,128)(2,1)S(1)}, u32[]{:S(2)}, u32[]{:S(2)}) async-start(bf16[128,32,256]{2,1,0:T(8,128)(2,1)} %bitcast.13), calls=%async_computation.2 | async-start | bytes 4194304 | tf_op jit(solution)/shard_map/all_to_all | solution.py:456
  105.6 43.9 %events_step.1 = bf16[6144,128]{1,0:T(8,128)(2,1)} custom-call(s32[10240]{0:T(1024)} %reshape.64.nbr_ref, bf16[8192,256]{1,0:T(8,128)(2,1)} %bitcast.3.rows_ref, f32[10,1024]{1,0:T(8,128)} %convert_bitcast_fusion.spacing_ref, f32[128,1]{1,0:T(8,128)} %copy.25.freq_ref, bf16[1024,256]{1,0:T(8,128)(2,1)} %get-tuple-element.24.mem_src_ref, ...), custom_call_target="tpu_custom_call" | custom-call | flops 48399998976 | bytes 132000000 | tf_op jit(solution)/shard_map/events_step/pallas_call | solution.py:303
  149.5 0.0 all-to-all-done.2
  149.5 35.1 %all_to_all.47.parts_ref = bf16[128,48,128]{2,1,0:T(8,128)(2,1)} all-to-all(bf16[128,48,128]{2,1,0:T(8,128)(2,1)} %bitcast.25), channel_id=1, replica_groups=mesh['node'=32,'rep'=4] {'node','rep'}, dimensions={0} | all-to-all | bytes 3145728 | tf_op jit(solution)/shard_map/all_to_all | solution.py:463
  184.6 2.9 %total_parts.1 = bf16[128,48,128]{2,1,0:T(8,128)(2,1)} custom-call(bf16[128,48,128]{2,1,0:T(8,128)(2,1)} %all_to_all.47.parts_ref), custom_call_target="tpu_custom_call" | custom-call | flops 3300000000 | bytes 9000000 | tf_op jit(solution)/shard_map/total_parts/pallas_call | solution.py:395
  187.5 3.8 %all-to-all-start.4 = ((bf16[128,48,128]{2,1,0:T(8,128)(2,1)}), bf16[128,48,128]{2,1,0:T(8,128)(2,1)S(1)}, u32[]{:S(2)}, u32[]{:S(2)}) async-start(bf16[128,48,128]{2,1,0:T(8,128)(2,1)} %total_parts.1), calls=%async_computation.4 | async-start | bytes 3145728 | tf_op jit(solution)/shard_map/all_to_all | solution.py:465
  191.3 12.1 %merge_rows.1 = bf16[4096,256]{1,0:T(8,128)(2,1)} custom-call(s32[1]{0:T(128)} %bitcast.place_ref, s32[4096]{0:T(1024)} %reshape.63.index_ref, bf16[4096,256]{1,0:T(8,128)(2,1)} %bitcast.23, bf16[4096,256]{1,0:T(8,128)(2,1)} %memory_ref.1), custom_call_target="tpu_custom_call" | custom-call | flops 12099999744 | bytes 33000000 | tf_op jit(solution)/shard_map/merge_rows/pallas_call | solution.py:373
  203.4 13.2 %all-to-all-done.4 = bf16[128,48,128]{2,1,0:T(8,128)(2,1)S(1)} async-done(((bf16[128,48,128]{2,1,0:T(8,128)(2,1)}), bf16[128,48,128]{2,1,0:T(8,128)(2,1)S(1)}, u32[]{:S(2)}, u32[]{:S(2)}) %all-to-all-start.4) | async-done | bytes 1572896 | tf_op jit(solution)/shard_map/all_to_all | solution.py:465
  216.7 1.2 copy-done.1
  217.8 3.0 %unpack_grads.1 = (f32[256,768]{1,0:T(8,128)}, f32[256,768]{1,0:T(8,128)}, f32[128,256]{1,0:T(8,128)}, f32[256,256]{1,0:T(8,128)}, f32[256,256]{1,0:T(8,128)}, /*index=5*/f32[256,256]{1,0:T(8,128)}, f32[256,256]{1,0:T(8,128)}) custom-call(bf16[6144,128]{1,0:T(8,128)(2,1)} %bitcast.24), custom_call_target="tpu_custom_call" | custom-call | flops 3300000000 | bytes 9000000 | tf_op jit(solution)/shard_map/unpack_grads/pallas_call | solution.py:416
  (11 shorter events, 0.0 us)
Async XLA Ops:
  31.1 5.0 %copy-start.2 = (s32[32,1,256]{2,1,0:T(1,128)S(1)}, s32[32,1,256]{2,1,0:T(1,128)}, u32[]{:S(2)}) copy-start(s32[32,1,256]{2,1,0:T(1,128)} %all_to_all.46) | copy-start | bytes 98308
  31.1 9.9 %copy-start.3 = (s32[1024,10]{0,1:T(8,128)S(1)}, s32[1024,10]{0,1:T(8,128)}, u32[]{:S(2)}) copy-start(s32[1024,10]{0,1:T(8,128)} %param.22) | copy-start | bytes 122884
  31.1 9.9 %copy-start.5 = (s32[1024]{0:T(1024)S(1)}, s32[1024]{0:T(1024)}, u32[]{:S(2)}) copy-start(s32[1024]{0:T(1024)} %param.21) | copy-start | bytes 12292
  31.2 10.5 %copy-start.6 = (f32[128]{0:T(128)S(1)}, f32[128]{0:T(128)}, u32[]{:S(2)}) copy-start(f32[128]{0:T(128)} %param.23) | copy-start | bytes 1540
  31.2 11.3 %copy-start.4 = (s32[1024,10]{0,1:T(8,128)S(1)}, s32[1024,10]{0,1:T(8,128)}, u32[]{:S(2)}) copy-start(s32[1024,10]{0,1:T(8,128)} %param.20) | copy-start | bytes 122884
  31.2 55.3 %all-to-all-start.1 = ((bf16[32,256,256]{2,1,0:T(8,128)(2,1)}), bf16[32,256,256]{2,1,0:T(8,128)(2,1)}, u32[]{:S(2)}, u32[]{:S(2)}) async-start(bf16[32,256,256]{2,1,0:T(8,128)(2,1)} %bitcast.22), calls=%async_computation.1 | async-start | bytes 8388608 | tf_op jit(solution)/shard_map/all_to_all | solution.py:441
  36.2 6.9 %collective-permute-start = (s32[32,32]{1,0:T(8,128)S(1)}, s32[32,32]{1,0:T(8,128)S(1)}, u32[]{:S(2)}, u32[]{:S(2)}) collective-permute-start(s32[32,32]{1,0:T(8,128)S(1)} %get-tuple-element.37), channel_id=1, source_target_pairs={{0,1},{1,2},{2,3},{3,0},{4,5},{5,6},{6,7},{7,4},{8,9},{9,10},{10,1... | collective-permute-start | bytes 12296 | tf_op jit(solution)/shard_map/ppermute | solution.py:445
  37.4 5.6 %collective-permute-start.1 = (s32[32,32]{1,0:T(8,128)S(1)}, s32[32,32]{1,0:T(8,128)S(1)}, u32[]{:S(2)}, u32[]{:S(2)}) collective-permute-start(s32[32,32]{1,0:T(8,128)S(1)} %get-tuple-element.37), channel_id=1, source_target_pairs={{0,2},{1,3},{2,0},{3,1},{4,6},{5,7},{6,4},{7,5},{8,10},{9,11},{10,... | collective-permute-start | bytes 12296 | tf_op jit(solution)/shard_map/ppermute | solution.py:445
  39.9 3.2 %collective-permute-start.2 = (s32[32,32]{1,0:T(8,128)S(1)}, s32[32,32]{1,0:T(8,128)S(1)}, u32[]{:S(2)}, u32[]{:S(2)}) collective-permute-start(s32[32,32]{1,0:T(8,128)S(1)} %get-tuple-element.37), channel_id=1, source_target_pairs={{0,3},{1,0},{2,1},{3,2},{4,7},{5,4},{6,5},{7,6},{8,11},{9,8},{10,9... | collective-permute-start | bytes 12296 | tf_op jit(solution)/shard_map/ppermute | solution.py:445
  97.6 51.9 %all-to-all-start.2 = ((bf16[128,32,256]{2,1,0:T(8,128)(2,1)}), bf16[128,32,256]{2,1,0:T(8,128)(2,1)S(1)}, u32[]{:S(2)}, u32[]{:S(2)}) async-start(bf16[128,32,256]{2,1,0:T(8,128)(2,1)} %bitcast.13), calls=%async_computation.2 | async-start | bytes 4194304 | tf_op jit(solution)/shard_map/all_to_all | solution.py:456
  149.5 38.0 %copy-start = (bf16[128,32,256]{2,1,0:T(8,128)(2,1)}, bf16[128,32,256]{2,1,0:T(8,128)(2,1)S(1)}, u32[]{:S(2)}) copy-start(bf16[128,32,256]{2,1,0:T(8,128)(2,1)S(1)} %all-to-all-done.2) | copy-start | bytes 6291460
  187.5 29.2 %all-to-all-start.4 = ((bf16[128,48,128]{2,1,0:T(8,128)(2,1)}), bf16[128,48,128]{2,1,0:T(8,128)(2,1)S(1)}, u32[]{:S(2)}, u32[]{:S(2)}) async-start(bf16[128,48,128]{2,1,0:T(8,128)(2,1)} %total_parts.1), calls=%async_computation.4 | async-start | bytes 3145728 | tf_op jit(solution)/shard_map/all_to_all | solution.py:465
  216.7 1.2 copy-start.1

commit v3 on v2

v3 whole, which is shorter than its diff:
```python
import functools
import math

import jax
import jax.numpy as jnp
from jax import lax
from jax.experimental import pallas as pl
from jax.experimental.pallas import tpu as pltpu
from jax.sharding import PartitionSpec as P

HEADS = 8
UCAP = 32
F32 = jnp.float32
BF16 = jnp.bfloat16
VMEM = pl.BlockSpec(memory_space=pltpu.VMEM)
SMEM = pl.BlockSpec(memory_space=pltpu.SMEM)
LIMIT = 58 * 1024 * 1024


def cost(micros):
    return pl.CostEstimate(flops=int(micros * 1.1e9), bytes_accessed=int(micros * 3.0e6), transcendentals=0)


def dot(a, b):
    return jnp.dot(a, b, preferred_element_type=F32)


def dot_nt(a, b):
    return lax.dot_general(a, b, (((1,), (1,)), ((), ())), preferred_element_type=F32)


def dot_tn(a, b):
    return lax.dot_general(a, b, (((0,), (0,)), ((), ())), preferred_element_type=F32)


def spread_table(rows_ref, table, base, step):
    count = rows_ref.shape[0]

    def body(i, carry):
        block = rows_ref[pl.ds(pl.multiple_of(i * step, step), step), :].astype(F32)
        start = base + i * (2 * step)
        table[pl.ds(start, step, stride=2), :] = block[:, :128]
        table[pl.ds(start + 1, step, stride=2), :] = block[:, 128:]
        return carry

    lax.fori_loop(0, count // step, body, 0)


def pick_rows(index_ref, offset, table, stage, count, start=0):
    for r in range(start, start + count):
        spot = index_ref[offset + r]
        stage[2 * r : 2 * r + 2, :] = table[pl.ds(pl.multiple_of(spot, 2), 2), :]


def joined(stage, start, count):
    left = stage[pl.ds(2 * start, count, stride=2), :]
    right = stage[pl.ds(2 * start + 1, count, stride=2), :]
    return jnp.concatenate([left, right], axis=1)


def serve_kernel(index_ref, rows_ref, out_ref, table, stage):
    block = pl.program_id(0)
    step = stage.shape[0] // 2
    count = out_ref.shape[0]

    @pl.when(block == 0)
    def _():
        spread_table(rows_ref, table, 0, 256)

    def body(i, carry):
        base = pl.multiple_of(i * step, step)
        pick_rows(index_ref, block * count + base, table, stage, step)
        out_ref[pl.ds(base, step), :] = joined(stage, 0, step).astype(BF16)
        return carry

    lax.fori_loop(0, count // step, body, 0)


def serve(index, memory):
    count = index.shape[0]
    rows, width = memory.shape
    blocks = 4
    return pl.pallas_call(
        serve_kernel,
        out_shape=jax.ShapeDtypeStruct((count, width), BF16),
        grid=(blocks,),
        in_specs=[SMEM, VMEM],
        out_specs=pl.BlockSpec((count // blocks, width), lambda i: (i, 0)),
        scratch_shapes=[pltpu.VMEM((2 * rows, 128), F32), pltpu.VMEM((256, 128), F32)],
        compiler_params=pltpu.CompilerParams(vmem_limit_bytes=LIMIT),
        cost_estimate=cost(11),
        name="serve_rows",
    )(index, memory)


def sigmoid(x):
    return 1.0 / (1.0 + jnp.exp(-x))


def gru_forward(mem_src, mem_dst, w_input_ref, w_hidden_ref):
    width = mem_src.shape[1]
    parts_in = [dot(mem_dst, w_input_ref[:, k * width : (k + 1) * width]) for k in range(3)]
    parts_hid = [dot(mem_src, w_hidden_ref[:, k * width : (k + 1) * width]) for k in range(3)]
    reset = sigmoid(parts_in[0] + parts_hid[0])
    update = sigmoid(parts_in[1] + parts_hid[1])
    candidate = jnp.tanh(parts_in[2] + reset * parts_hid[2])
    rows = mem_src.astype(F32)
    hidden = (1.0 - update) * candidate + update * rows
    return rows, reset, update, candidate, parts_hid[2], hidden


def memory_kernel(
    src_ref, dst_ref, src_row_ref, rows_ref, w_input_ref, w_hidden_ref,
    mem_src_ref, mem_dst_ref, change_ref, table, stage, delta,
):
    spread_table(rows_ref, table, 0, 256)
    step = stage.shape[0] // 4
    events = mem_src_ref.shape[0]

    def body(i, carry):
        base = pl.multiple_of(i * step, step)
        pick_rows(src_ref, base, table, stage, step)
        pick_rows(dst_ref, base, table, stage.at[pl.ds(2 * step, 2 * step)], step)
        mem_src = joined(stage, 0, step).astype(BF16)
        mem_dst = joined(stage, step, step).astype(BF16)
        mem_src_ref[pl.ds(base, step), :] = mem_src
        mem_dst_ref[pl.ds(base, step), :] = mem_dst
        rows, _, _, _, _, hidden = gru_forward(mem_src, mem_dst, w_input_ref, w_hidden_ref)
        delta[pl.ds(base, step), :] = (hidden - rows).astype(BF16)
        return carry

    lax.fori_loop(0, events // step, body, 0)
    source = src_row_ref[...]
    slot = (source >> 8) * UCAP + (source & 255)
    reps, block_width = change_ref.shape[1], change_ref.shape[3]
    slots = change_ref.shape[0] * UCAP
    part = 256
    for k in range(slots // part):
        ids = lax.broadcasted_iota(jnp.int32, (part, events), 0) + k * part
        picked = jnp.where(ids == slot, 1.0, 0.0).astype(BF16)
        block = dot(picked, delta[...]).astype(BF16).reshape(part // UCAP, 1, UCAP, block_width)
        owners = pl.ds(k * (part // UCAP), part // UCAP)
        change_ref[owners] = jnp.broadcast_to(block, (part // UCAP, reps, UCAP, block_width))


def memory_step(src_slot, dst_slot, fetched, w_input, w_hidden, reps):
    events = src_slot.shape[0]
    count, width = fetched.shape
    owners = count // 256
    return pl.pallas_call(
        memory_kernel,
        out_shape=(
            jax.ShapeDtypeStruct((events, width), BF16),
            jax.ShapeDtypeStruct((events, width), BF16),
            jax.ShapeDtypeStruct((owners, reps, UCAP, width), BF16),
        ),
        in_specs=[SMEM, SMEM, VMEM, VMEM, VMEM, VMEM],
        out_specs=(VMEM, VMEM, VMEM),
        scratch_shapes=[
            pltpu.VMEM((2 * count, 128), F32),
            pltpu.VMEM((512, 128), F32),
            pltpu.VMEM((events, width), BF16),
        ],
        compiler_params=pltpu.CompilerParams(vmem_limit_bytes=LIMIT),
        cost_estimate=cost(8),
        name="memory_step",
    )(2 * src_slot, 2 * dst_slot, src_slot.reshape(1, events), fetched, w_input, w_hidden)


COS_TERMS = (
    1.0,
    -0.49999988079071045,
    0.041666485369205475,
    -0.001388777862302959,
    2.4769342417130247e-05,
    -2.7073761543761066e-07,
    1.7225967319234314e-09,
)
TURN_HIGH = 6.28125
TURN_LOW = 2.0 * math.pi - 6.28125


def cosine(x):
    turns = jnp.floor(x * (0.5 / math.pi) + 0.5)
    rest = (x - turns * TURN_HIGH) - turns * TURN_LOW
    square = rest * rest
    total = jnp.full_like(x, COS_TERMS[-1])
    for term in COS_TERMS[-2::-1]:
        total = total * square + term
    return total


GROUP = 16


def phase_kernel(spacing_ref, freq_ref, w_time_ref, phase_ref, timed_ref):
    wave = cosine(freq_ref[...] * spacing_ref[...]).astype(BF16)
    phase_ref[...] = wave
    timed_ref[...] = dot_tn(wave, w_time_ref[...]).astype(BF16)


def phase_step(spacing, frequency, w_time):
    total = spacing.shape[1]
    freqs, width = w_time.shape
    step = 1024
    return pl.pallas_call(
        phase_kernel,
        out_shape=(
            jax.ShapeDtypeStruct((freqs, total), BF16),
            jax.ShapeDtypeStruct((total, width), BF16),
        ),
        grid=(total // step,),
        in_specs=[
            pl.BlockSpec((1, step), lambda i: (0, i)),
            pl.BlockSpec((freqs, 1), lambda i: (0, 0)),
            pl.BlockSpec((freqs, width), lambda i: (0, 0)),
        ],
        out_specs=(
            pl.BlockSpec((freqs, step), lambda i: (0, i)),
            pl.BlockSpec((step, width), lambda i: (i, 0)),
        ),
        compiler_params=pltpu.CompilerParams(vmem_limit_bytes=LIMIT),
        cost_estimate=cost(10),
        name="phase_step",
    )(spacing, frequency.reshape(freqs, 1), w_time)


def events_kernel(
    nbr_ref, rows_ref, phase_ref, timed_ref, mem_src_ref, mem_dst_ref, slope_ref,
    w_input_ref, w_hidden_ref, w_time_ref, w_query_ref, w_key_ref, w_value_ref, w_out_ref,
    grads_ref,
    rows_in, phase, timed, table, stage, ones, mixed, keys, values, score, dprob, slopes,
    hidden_half, query, dattended, reset, update, candidate, hid_c, attended, dquery,
    acc_time, acc_kv, both_weights, dmixed, row_sems, time_sems, phase_sem,
):
    events, width = slope_ref.shape
    nbrs = nbr_ref.shape[0] // events
    flat = stage.shape[0] // 2
    size = flat // nbrs
    blocks = events // size
    large = dmixed.shape[0]
    head = width // HEADS
    scale = head ** -0.5
    chunks = row_sems.shape[0]
    part = rows_in.shape[0] // chunks
    row_copies = [
        pltpu.make_async_copy(
            rows_ref.at[pl.ds(c * part, part)], rows_in.at[pl.ds(c * part, part)], row_sems.at[c]
        )
        for c in range(chunks)
    ]

    def time_copy(c):
        length = nbrs * events // time_sems.shape[0]
        span = pl.ds(pl.multiple_of(c * length, length), length)
        return pltpu.make_async_copy(timed_ref.at[span], timed.at[span], time_sems.at[c])

    for copy in row_copies:
        copy.start()
    for c in range(time_sems.shape[0]):
        time_copy(c).start()
    phase_copy = pltpu.make_async_copy(phase_ref, phase, phase_sem)
    phase_copy.start()
    row_id = lax.broadcasted_iota(jnp.int32, (width, width), 0) // head
    col_id = lax.broadcasted_iota(jnp.int32, (width, width), 1) // head
    ones[...] = jnp.where(row_id == col_id, 1.0, 0.0).astype(BF16)
    both_weights[:, :width] = w_key_ref[...]
    both_weights[:, width:] = w_value_ref[...]
    for ref in (acc_time, acc_kv):
        ref[...] = jnp.zeros_like(ref)

    def forward(i, carry):
        span = pl.ds(pl.multiple_of(i * 256, 256), 256)
        _, r, u, c, h, hidden = gru_forward(mem_src_ref[span, :], mem_dst_ref[span, :], w_input_ref, w_hidden_ref)
        reset[span, :] = r
        update[span, :] = u
        candidate[span, :] = c
        hid_c[span, :] = h
        half = hidden.astype(BF16)
        hidden_half[span, :] = half
        query[span, :] = dot(half, w_query_ref[...]).astype(BF16)
        dattended[span, :] = dot_nt(slope_ref[span, :], w_out_ref[...]).astype(BF16)
        return carry

    lax.fori_loop(0, events // 256, forward, 0)
    for c in range(chunks):
        row_copies[c].wait()
        spread_table(rows_in.at[pl.ds(c * part, part)], table, 2 * c * part, 256)
    pick_rows(nbr_ref, 0, table, stage, flat)
    def body(i, carry):
        at = pl.multiple_of(i * flat, flat)
        event = pl.multiple_of(i * size, size)
        wave_part = nbrs * events // time_sems.shape[0]

        @pl.when(lax.rem(at, wave_part) == 0)
        def _():
            time_copy(at // wave_part).wait()

        rows = (joined(stage, 0, flat) + timed[pl.ds(at, flat), :].astype(F32)).astype(BF16)
        mixed[pl.ds(at, flat), :] = rows
        key = dot(rows, w_key_ref[...]).astype(BF16)
        value = dot(rows, w_value_ref[...]).astype(BF16)
        keys[...] = key
        values[...] = value
        key_side, value_side = [], []
        for g in range(size // GROUP):
            own = pl.ds(event + g * GROUP, GROUP)
            one_query, one_slope = query[own, :], dattended[own, :]
            for j in range(nbrs):
                span = slice((g * nbrs + j) * GROUP, (g * nbrs + j + 1) * GROUP)
                key_side.append(key[span, :] * one_query)
                value_side.append(value[span, :] * one_slope)
        score[...] = dot(jnp.concatenate(key_side, axis=0), ones[...])
        dprob[...] = dot(jnp.concatenate(value_side, axis=0), ones[...])
        upcoming = jnp.minimum(i + 1, blocks - 1) * flat
        for g in range(size // GROUP):
            own = pl.ds(event + g * GROUP, GROUP)
            spans = [pl.ds((g * nbrs + j) * GROUP, GROUP) for j in range(nbrs)]
            scores = [score[span, :] for span in spans]
            top = functools.reduce(jnp.maximum, scores)
            weights = [jnp.exp2((s - top) * (scale * math.log2(math.e))) for s in scores]
            total = functools.reduce(jnp.add, weights)
            inverse = 1.0 / total
            outcome, overlap = jnp.zeros_like(top), jnp.zeros_like(top)
            for j in range(nbrs):
                outcome = outcome + weights[j] * values[spans[j], :].astype(F32)
                overlap = overlap + weights[j] * dprob[spans[j], :]
                pick_rows(nbr_ref, upcoming, table, stage, GROUP // 2, (g * nbrs + j) * GROUP)
            overlap = overlap * inverse
            attended[own, :] = (outcome * inverse).astype(BF16)
            datt = dattended[own, :].astype(F32)
            asked = query[own, :].astype(F32) * scale
            change = jnp.zeros_like(top)
            for j in range(nbrs):
                span = spans[j]
                prob = weights[j] * inverse
                dscore = prob * (dprob[span, :] - overlap)
                change = change + dscore * keys[span, :].astype(F32)
                here = pl.ds(at + (g * nbrs + j) * GROUP, GROUP)
                slopes[here, :width] = (dscore * asked).astype(BF16)
                slopes[here, width:] = (prob * datt).astype(BF16)
                pick_rows(nbr_ref, upcoming, table, stage, GROUP // 2, (g * nbrs + j) * GROUP + GROUP // 2)
            dquery[own, :] = (change * scale).astype(BF16)
        return carry

    lax.fori_loop(0, blocks, body, 0)

    phase_copy.wait()
    for i in range(nbrs * events // large):
        for k in range(large // 256):
            span = slice(i * large + k * 256, i * large + (k + 1) * 256)
            dmixed[k * 256 : (k + 1) * 256, :] = dot_nt(slopes[span, :], both_weights[...]).astype(BF16)
        span = slice(i * large, (i + 1) * large)
        acc_time[...] += dot(phase[:, span], dmixed[...])
        acc_kv[...] += dot_tn(mixed[span, :], slopes[span, :])
    total_rows = 0

    def write(value):
        nonlocal total_rows
        depth, columns = value.shape
        for k in range(columns // 128):
            grads_ref[total_rows : total_rows + depth, :] = value[:, k * 128 : (k + 1) * 128].astype(BF16)
            total_rows += depth

    mem_src, mem_dst, slope = mem_src_ref[...], mem_dst_ref[...], slope_ref[...]
    rows = mem_src.astype(F32)
    dhidden = slope.astype(F32) + dot_nt(dquery[...], w_query_ref[...])
    u, c, r = update[...], candidate[...], reset[...]
    dcand = dhidden * (1.0 - u) * (1.0 - c * c)
    dupdate = (dhidden * (rows - c) * u * (1.0 - u)).astype(BF16)
    dreset = (dcand * hid_c[...] * r * (1.0 - r)).astype(BF16)
    for piece in (dreset, dupdate, dcand.astype(BF16)):
        write(dot_tn(mem_dst, piece))
    for piece in (dreset, dupdate, (dcand * r).astype(BF16)):
        write(dot_tn(mem_src, piece))
    write(acc_time[...])
    write(dot_tn(hidden_half[...], dquery[...]))
    write(acc_kv[...])
    write(dot_tn(attended[...], slope))
    if total_rows < grads_ref.shape[0]:
        grads_ref[total_rows:, :] = jnp.zeros((grads_ref.shape[0] - total_rows, 128), BF16)


def events_step(nbr_index, fetched, phase, timed, mem_src, mem_dst, slope, weights, grad_rows, size=64):
    events, width = slope.shape
    nbrs = nbr_index.shape[0] // events
    count = fetched.shape[0]
    freqs = phase.shape[0]
    flat = nbrs * size
    anywhere = pl.BlockSpec(memory_space=pl.ANY)
    halves = pltpu.VMEM((events, width), BF16)
    wholes = pltpu.VMEM((events, width), F32)
    return pl.pallas_call(
        events_kernel,
        out_shape=jax.ShapeDtypeStruct((grad_rows, 128), BF16),
        in_specs=[SMEM, anywhere, anywhere, anywhere] + [VMEM] * 10,
        out_specs=VMEM,
        scratch_shapes=[
            pltpu.VMEM((count, width), BF16),
            pltpu.VMEM((freqs, nbrs * events), BF16),
            pltpu.VMEM((nbrs * events, width), BF16),
            pltpu.VMEM((2 * count, 128), F32),
            pltpu.VMEM((2 * flat, 128), F32),
            pltpu.VMEM((width, width), BF16),
            pltpu.VMEM((nbrs * events, width), BF16),
            pltpu.VMEM((flat, width), BF16),
            pltpu.VMEM((flat, width), BF16),
            pltpu.VMEM((flat, width), F32),
            pltpu.VMEM((flat, width), F32),
            pltpu.VMEM((nbrs * events, 2 * width), BF16),
            halves, halves, halves, wholes, wholes, wholes, wholes, halves, halves,
            pltpu.VMEM((freqs, width), F32),
            pltpu.VMEM((width, 2 * width), F32),
            pltpu.VMEM((width, 2 * width), BF16),
            pltpu.VMEM((2560, width), BF16),
            pltpu.SemaphoreType.DMA((8,)),
            pltpu.SemaphoreType.DMA((4,)),
            pltpu.SemaphoreType.DMA,
        ],
        compiler_params=pltpu.CompilerParams(vmem_limit_bytes=LIMIT),
        cost_estimate=cost(40),
        name="events_step",
    )(nbr_index, fetched, phase, timed, mem_src, mem_dst, slope, *weights)


def merge_kernel(place_ref, index_ref, change_ref, memory_ref, out_ref, table, stage):
    rows = memory_ref.shape[0]
    spread_table(memory_ref, table, 0, 256)
    step = stage.shape[0] // 2
    group = UCAP
    reps = 4
    owner_rows = change_ref.shape[0] // reps
    here = place_ref[0]

    def body(i, carry):
        base = pl.multiple_of(i * step, step)
        block = change_ref[pl.ds(base, step), :].astype(F32)
        stage[pl.ds(0, step, stride=2), :] = block[:, :128]
        stage[pl.ds(1, step, stride=2), :] = block[:, 128:]
        for g in range(step // group):
            sender = i * (step // group) + g
            first = lax.rem(here - lax.rem(sender, reps) + reps, reps) * owner_rows + sender // reps * group
            spots = [pl.ds(pl.multiple_of(index_ref[first + r], 2), 2) for r in range(group)]
            sums = [
                table[spots[r], :] + stage[2 * (g * group + r) : 2 * (g * group + r) + 2, :]
                for r in range(group)
            ]
            for r in range(group):
                table[spots[r], :] = sums[r]
        return carry

    lax.fori_loop(0, change_ref.shape[0] // step, body, 0)

    def finish(i, carry):
        base = pl.multiple_of(i * 256, 256)
        left = table[pl.ds(2 * base, 256, stride=2), :]
        right = table[pl.ds(2 * base + 1, 256, stride=2), :]
        out_ref[pl.ds(base, 256), :] = jnp.concatenate([left, right], axis=1).astype(BF16)
        return carry

    lax.fori_loop(0, rows // 256, finish, 0)


def merge(place, index, change, memory):
    rows, width = memory.shape
    return pl.pallas_call(
        merge_kernel,
        out_shape=jax.ShapeDtypeStruct((rows, width), BF16),
        in_specs=[SMEM, SMEM, VMEM, VMEM],
        out_specs=VMEM,
        scratch_shapes=[pltpu.VMEM((2 * rows, 128), F32), pltpu.VMEM((256, 128), F32)],
        compiler_params=pltpu.CompilerParams(vmem_limit_bytes=LIMIT),
        cost_estimate=cost(11),
        name="merge_rows",
    )(place, index, change, memory)


def total_kernel(parts_ref, out_ref):
    total = jnp.zeros(parts_ref.shape[1:], F32)
    for k in range(parts_ref.shape[0]):
        total = total + parts_ref[k].astype(F32)
    total = total.astype(BF16)
    for k in range(parts_ref.shape[0]):
        out_ref[k] = total


def total_parts(parts):
    return pl.pallas_call(
        total_kernel,
        out_shape=jax.ShapeDtypeStruct(parts.shape, BF16),
        in_specs=[VMEM],
        out_specs=VMEM,
        compiler_params=pltpu.CompilerParams(vmem_limit_bytes=8 * 1024 * 1024),
        cost_estimate=cost(3),
        name="total_parts",
    )(parts)


def unpack_kernel(flat_ref, *out_refs):
    row = 0
    for out_ref in out_refs:
        depth, columns = out_ref.shape
        for k in range(columns // 128):
            out_ref[:, k * 128 : (k + 1) * 128] = flat_ref[row : row + depth, :].astype(F32)
            row += depth


def unpack(flat, shapes):
    return pl.pallas_call(
        unpack_kernel,
        out_shape=tuple(jax.ShapeDtypeStruct(shape, F32) for shape in shapes),
        in_specs=[VMEM],
        out_specs=tuple(VMEM for _ in shapes),
        compiler_params=pltpu.CompilerParams(vmem_limit_bytes=12 * 1024 * 1024),
        cost_estimate=cost(3),
        name="unpack_grads",
    )(flat)


BOTH = ("node", "rep")


def local(
    memory, req_rows, src_slot, dst_slot, nbr_slot, event_time, nbr_time, frequency, emb_grad,
    w_input, w_hidden, w_time, w_query, w_key, w_value, w_out,
):
    weights = (w_input, w_hidden, w_time, w_query, w_key, w_value, w_out)
    requests = req_rows[0]
    owners, capacity = requests.shape
    width = memory.shape[1]
    reps = lax.axis_size("rep")
    doubled = lax.optimization_barrier((2 * requests).reshape(owners, capacity // 128, 128))
    asked = lax.all_to_all(doubled, "node", split_axis=0, concat_axis=0, tiled=True)
    asked = asked.reshape(owners, capacity)
    served = serve(asked.reshape(-1), memory).reshape(owners, capacity, width)
    fetched = lax.all_to_all(served, "node", split_axis=0, concat_axis=0, tiled=True)
    fetched = fetched.reshape(owners * capacity, width)
    lead = asked[:, :UCAP]
    turned = [lead] + [
        lax.ppermute(lead, "rep", [(i, (i + k) % reps) for i in range(reps)]) for k in range(1, reps)
    ]
    touched = jnp.stack(turned).reshape(-1)
    place = lax.axis_index("rep").astype(jnp.int32).reshape(1)
    events, nbrs = nbr_slot.shape
    nbr_index = (2 * nbr_slot).reshape(events // GROUP, GROUP, nbrs).transpose(0, 2, 1).reshape(-1)
    spacing = (event_time[:, None] - nbr_time).astype(F32)
    spacing = spacing.reshape(events // GROUP, GROUP, nbrs).transpose(0, 2, 1).reshape(1, -1)
    phase, timed = phase_step(spacing, frequency, w_time)
    fetched, touched, nbr_index, phase, timed = lax.optimization_barrier(
        (fetched, touched, nbr_index, phase, timed)
    )
    mem_src, mem_dst, change = memory_step(src_slot, dst_slot, fetched, w_input, w_hidden, reps)
    updates = lax.all_to_all(change.reshape(owners * reps * UCAP, width), BOTH, split_axis=0, concat_axis=0, tiled=True)
    shapes = (w_input.shape, w_hidden.shape, w_time.shape, w_query.shape, w_key.shape, w_value.shape, w_out.shape)
    used = sum(shape[0] * shape[1] for shape in shapes) // 128
    devices = owners * reps
    share = -(-used // (devices * 16)) * 16
    grads = events_step(nbr_index, fetched, phase, timed, mem_src, mem_dst, emb_grad, weights, devices * share)
    grads, updates = lax.optimization_barrier((grads, updates))
    parts = lax.all_to_all(grads, BOTH, split_axis=0, concat_axis=0, tiled=True)
    summed = total_parts(parts.reshape(devices, share, 128))
    flat = lax.all_to_all(summed.reshape(devices * share, 128), BOTH, split_axis=0, concat_axis=0, tiled=True)
    new_memory = merge(place, touched, updates, memory)
    return (new_memory, *unpack(flat, shapes))


def solution(mesh):
    split = P(BOTH)
    placed = (
        P("node", None), P(BOTH, None, None), split, split, P(BOTH, None), split, P(BOTH, None),
        P(), P(BOTH, None), P(), P(), P(), P(), P(), P(), P(),
    )
    return jax.shard_map(
        local,
        mesh=mesh,
        in_specs=placed,
        out_specs=(P("node", None), P(), P(), P(), P(), P(), P(), P()),
        check_vma=False,
    )
```

time: 222 us -> 203 us (0.914)
  waiting for transfers between devices: 56 us -> 46 us
  Pallas kernels: 83.5 us -> 76.7 us
  local copies, waits for them, and re-layouts: 6.67 us -> 3.72 us
    all_to_all x1, waiting for transfers between devices: 42.7 us -> 32 us  [local(): lax.all_to_all(served, 'node', split_axis=0, concat_axis=0, tiled=True)]
    pallas_call x1, Pallas kernels: 43.9 us -> 33.6 us  [events_step(): pl.pallas_call(events_kernel, out_shape=jax.ShapeDtypeStruct((grad_rows,...]
    pallas_call x0 -> x1, Pallas kernels: none -> 8.96 us  [phase_step(): pl.pallas_call(phase_kernel, out_shape=(jax.ShapeDtypeStruct((freqs, tota...]
    broadcast_in_dim x1 -> x0, local copies, waits for them, and re-layouts: 2.63 us -> none  [local(): jnp.broadcast_to(change.reshape(owners, 1, UCAP, width), (owners, reps, U...]
  transfers between devices with their start and end apart: 6 -> 6, of which waited for: 2 -> 3; matrix products, arithmetic and copies ran while one was open for 1% -> 2% of each run, Pallas kernels for 25% -> 27%
where the time goes in v3:
time: 203 us; the launch traced here: 202 us
  Pallas kernels  76.7 us (38%)
  blocking collectives  51.6 us (25%)
  waiting for transfers between devices  46 us (23%)
  starting transfers between devices  21.6 us (11%)
  local copies, waits for them, and re-layouts  3.72 us (2%)
    all_to_all x1, blocking collectives, local(): parts = lax.all_to_all(grads, BOTH, split_axis=0, concat_axis=0, tiled=True)  35 us
    pallas_call x1, Pallas kernels, events_step(): pl.pallas_call(events_kernel, out_shape=jax.ShapeDtypeStruct((grad_rows,...  33.6 us
    all_to_all x1, waiting for transfers between devices, local(): lax.all_to_all(served, 'node', split_axis=0, concat_axis=0, tiled=True)  32 us
    all_to_all x1, blocking collectives, local(): lax.all_to_all(doubled, 'node', split_axis=0, concat_axis=0, tiled=True)  16.7 us
    all_to_all x1, waiting for transfers between devices, local(): lax.all_to_all(summed.reshape(devices * share, 128), BOTH, split_axis=0,...  13.9 us
    pallas_call x1, Pallas kernels, merge(): pl.pallas_call(merge_kernel, out_shape=jax.ShapeDtypeStruct((rows, width)...  11.5 us
    pallas_call x1, Pallas kernels, serve(): pl.pallas_call(serve_kernel, out_shape=jax.ShapeDtypeStruct((count, width...  10.9 us
    pallas_call x1, Pallas kernels, phase_step(): pl.pallas_call(phase_kernel, out_shape=(jax.ShapeDtypeStruct((freqs, tota...  8.96 us
  transfers between devices with their start and end apart: 6, of which 3 were waited for; matrix products, arithmetic and copies ran while one was open for 2% of the time, Pallas kernels for 27%

profile of v3, /device:TPU:1, one launch (start us, length us, event | category | flops | bytes accessed | tf_op | source)
XLA Modules:
  0.0 201.8 jit_solution(16576390512272868484)
XLA Ops:
  0.6 0.8 broadcast_multiply_fusion.1
  1.4 16.7 %all_to_all.39 = s32[32,2,128]{2,1,0:T(2,128)} all-to-all(s32[32,2,128]{2,1,0:T(2,128)S(1)} %mul.24), channel_id=1, replica_groups=mesh['node'=32,'rep'=4] {'node'}, dimensions={0} | all-to-all | bytes 65536 | tf_op jit(solution)/shard_map/all_to_all | solution.py:533
  18.1 10.9 %serve_rows.1 = bf16[8192,256]{1,0:T(8,128)(2,1)} custom-call(s32[8192]{0:T(1024)} %bitcast.32, bf16[4096,256]{1,0:T(8,128)(2,1)} %memory_ref.1), custom_call_target="tpu_custom_call" | custom-call | flops 12099999744 | bytes 33000000 | tf_op jit(solution)/shard_map/serve_rows/pallas_call | solution.py:83
  29.0 4.9 %all-to-all-start.1 = ((bf16[32,256,256]{2,1,0:T(8,128)(2,1)}), bf16[32,256,256]{2,1,0:T(8,128)(2,1)}, u32[]{:S(2)}, u32[]{:S(2)}) async-start(bf16[32,256,256]{2,1,0:T(8,128)(2,1)} %bitcast.26), calls=%async_computation.1 | async-start | bytes 8388608 | tf_op jit(solution)/shard_map/all_to_all | solution.py:536
  34.0 0.1 reshape.73
  34.1 0.2 copy.27
  34.3 0.8 reshape.74.spacing_ref
  35.1 0.7 copy.28.freq_ref
  35.9 0.0 copy-start.5
  35.9 0.0 copy-start.6
  35.9 9.0 %phase_step.1 = (bf16[128,10240]{1,0:T(8,128)(2,1)}, bf16[10240,256]{1,0:T(8,128)(2,1)}) custom-call(f32[1,10240]{1,0:T(1,128)} %reshape.74.spacing_ref, f32[128,1]{1,0:T(8,128)} %copy.28.freq_ref, bf16[128,256]{1,0:T(8,128)(2,1)} %w_time_ref.3), custom_call_target="tpu_custom_call" | custom-call | flops 11000000512 | bytes 30000000 | tf_op jit(solution)/shard_map/phase_step/pallas_call | solution.py:206
  44.9 1.3 collective-permute-start
  46.2 2.4 %collective-permute-start.1 = (s32[32,32]{1,0:T(8,128)S(1)}, s32[32,32]{1,0:T(8,128)S(1)}, u32[]{:S(2)}, u32[]{:S(2)}) collective-permute-start(s32[32,32]{1,0:T(8,128)S(1)} %get-tuple-element.47), channel_id=1, source_target_pairs={{0,2},{1,3},{2,0},{3,1},{4,6},{5,7},{6,4},{7,5},{8,10},{9,11},{10,... | collective-permute-start | bytes 12296 | tf_op jit(solution)/shard_map/ppermute | solution.py:540
  48.6 1.1 collective-permute-start.2
  49.8 0.6 broadcast_multiply_fusion.2
  50.4 0.1 reshape.71
  50.5 0.2 copy.26
  50.7 0.8 reshape.72.nbr_ref
  51.5 0.0 collective-permute-done
  51.5 0.1 collective-permute-done.2
  51.6 0.7 reshape.70.index_ref
  52.3 32.0 %all-to-all-done.1 = bf16[32,256,256]{2,1,0:T(8,128)(2,1)} async-done(((bf16[32,256,256]{2,1,0:T(8,128)(2,1)}), bf16[32,256,256]{2,1,0:T(8,128)(2,1)}, u32[]{:S(2)}, u32[]{:S(2)}) %all-to-all-start.1) | async-done | bytes 4194336 | tf_op jit(solution)/shard_map/all_to_all | solution.py:536
  84.3 8.7 %memory_step.1 = (bf16[1024,256]{1,0:T(8,128)(2,1)}, bf16[1024,256]{1,0:T(8,128)(2,1)}, bf16[32,4,32,256]{3,2,1,0:T(8,128)(2,1)}) custom-call(s32[1024]{0:T(1024)} %get-tuple-element.49.src_ref, s32[1024]{0:T(1024)} %get-tuple-element.48.dst_ref, s32[1,1024]{1,0:T(1,128)} %bitcast.38, bf16[8192,256]{1,0:T(8,128)(2,1)} %bitcast.3.rows_ref, ...), custom_call_target="tpu_custom_call" | custom-call | flops 8800000000 | bytes 24000000 | tf_op jit(solution)/shard_map/memory_step/pallas_call | solution.py:150
  93.1 7.9 %all-to-all-start.2 = ((bf16[128,32,256]{2,1,0:T(8,128)(2,1)}), bf16[128,32,256]{2,1,0:T(8,128)(2,1)S(1)}, u32[]{:S(2)}, u32[]{:S(2)}) async-start(bf16[128,32,256]{2,1,0:T(8,128)(2,1)} %bitcast.28), calls=%async_computation.2 | async-start | bytes 4194304 | tf_op jit(solution)/shard_map/all_to_all | solution.py:553
  101.0 33.6 %events_step.1 = bf16[6144,128]{1,0:T(8,128)(2,1)} custom-call(s32[10240]{0:T(1024)} %reshape.72.nbr_ref, bf16[8192,256]{1,0:T(8,128)(2,1)} %bitcast.3.rows_ref, bf16[128,10240]{1,0:T(8,128)(2,1)} %get-tuple-element.32.phase_ref, bf16[10240,256]{1,0:T(8,128)(2,1)} %get-tuple-element.33.timed_ref, bf16[1024,256]{1,0:T(8,128)(2,1)} %get-tuple-element.34.mem_src_ref, ...), custom_call_target="tpu_custom_call" | custom-call | flops 44000002048 | bytes 120000000 | tf_op jit(solution)/shard_map/events_step/pallas_call | solution.py:393
  134.6 0.0 all-to-all-done.2
  134.6 35.0 %all_to_all.40.parts_ref = bf16[128,48,128]{2,1,0:T(8,128)(2,1)S(1)} all-to-all(bf16[128,48,128]{2,1,0:T(8,128)(2,1)} %bitcast.29), channel_id=1, replica_groups=mesh['node'=32,'rep'=4] {'node','rep'}, dimensions={0} | all-to-all | bytes 3145728 | tf_op jit(solution)/shard_map/all_to_all | solution.py:560
  169.6 1.5 total_parts.1
  171.1 3.8 %all-to-all-start.4 = ((bf16[128,48,128]{2,1,0:T(8,128)(2,1)}), bf16[128,48,128]{2,1,0:T(8,128)(2,1)S(1)}, u32[]{:S(2)}, u32[]{:S(2)}) async-start(bf16[128,48,128]{2,1,0:T(8,128)(2,1)} %total_parts.1), calls=%async_computation.4 | async-start | bytes 3145728 | tf_op jit(solution)/shard_map/all_to_all | solution.py:562
  174.9 11.5 %merge_rows.1 = bf16[4096,256]{1,0:T(8,128)(2,1)} custom-call(s32[1]{0:T(128)} %bitcast.place_ref, s32[4096]{0:T(1024)} %reshape.70.index_ref, bf16[4096,256]{1,0:T(8,128)(2,1)} %bitcast.27, bf16[4096,256]{1,0:T(8,128)(2,1)} %memory_ref.1), custom_call_target="tpu_custom_call" | custom-call | flops 12099999744 | bytes 33000000 | tf_op jit(solution)/shard_map/merge_rows/pallas_call | solution.py:466
  186.4 13.9 %all-to-all-done.4 = bf16[128,48,128]{2,1,0:T(8,128)(2,1)S(1)} async-done(((bf16[128,48,128]{2,1,0:T(8,128)(2,1)}), bf16[128,48,128]{2,1,0:T(8,128)(2,1)S(1)}, u32[]{:S(2)}, u32[]{:S(2)}) %all-to-all-start.4) | async-done | bytes 1572896 | tf_op jit(solution)/shard_map/all_to_all | solution.py:562
  200.3 1.6 unpack_grads.1
  (21 shorter events, 0.1 us)
Async XLA Ops:
  29.0 5.0 %copy-start.2 = (s32[1024,10]{0,1:T(8,128)S(1)}, s32[1024,10]{0,1:T(8,128)}, u32[]{:S(2)}) copy-start(s32[1024,10]{0,1:T(8,128)} %param.22) | copy-start | bytes 122884
  29.0 5.0 %copy-start.4 = (s32[1024]{0:T(1024)S(1)}, s32[1024]{0:T(1024)}, u32[]{:S(2)}) copy-start(s32[1024]{0:T(1024)} %param.21) | copy-start | bytes 12292
  29.0 6.1 %copy-start.7 = (f32[128]{0:T(128)S(1)}, f32[128]{0:T(128)}, u32[]{:S(2)}) copy-start(f32[128]{0:T(128)} %param.23) | copy-start | bytes 1540
  29.0 6.9 %copy-start.3 = (s32[1024,10]{0,1:T(8,128)S(1)}, s32[1024,10]{0,1:T(8,128)}, u32[]{:S(2)}) copy-start(s32[1024,10]{0,1:T(8,128)} %param.20) | copy-start | bytes 122884
  29.0 55.3 %all-to-all-start.1 = ((bf16[32,256,256]{2,1,0:T(8,128)(2,1)}), bf16[32,256,256]{2,1,0:T(8,128)(2,1)}, u32[]{:S(2)}, u32[]{:S(2)}) async-start(bf16[32,256,256]{2,1,0:T(8,128)(2,1)} %bitcast.26), calls=%async_computation.1 | async-start | bytes 8388608 | tf_op jit(solution)/shard_map/all_to_all | solution.py:536
  35.9 9.0 %copy-start.1 = (s32[32,2,128]{2,1,0:T(2,128)S(1)}, s32[32,2,128]{2,1,0:T(2,128)}, u32[]{:S(2)}) copy-start(s32[32,2,128]{2,1,0:T(2,128)} %all_to_all.39) | copy-start | bytes 98308
  35.9 13.9 %copy-start.5 = (s32[1024]{0:T(1024)S(1)}, s32[1024]{0:T(1024)}, u32[]{:S(2)}) copy-start(s32[1024]{0:T(1024)} %param.19) | copy-start | bytes 12292
  35.9 13.9 %copy-start.6 = (s32[1024]{0:T(1024)S(1)}, s32[1024]{0:T(1024)}, u32[]{:S(2)}) copy-start(s32[1024]{0:T(1024)} %param.18) | copy-start | bytes 12292
  44.9 6.6 %collective-permute-start = (s32[32,32]{1,0:T(8,128)S(1)}, s32[32,32]{1,0:T(8,128)S(1)}, u32[]{:S(2)}, u32[]{:S(2)}) collective-permute-start(s32[32,32]{1,0:T(8,128)S(1)} %get-tuple-element.47), channel_id=1, source_target_pairs={{0,1},{1,2},{2,3},{3,0},{4,5},{5,6},{6,7},{7,4},{8,9},{9,10},{10,1... | collective-permute-start | bytes 12296 | tf_op jit(solution)/shard_map/ppermute | solution.py:540
  46.2 5.3 %collective-permute-start.1 = (s32[32,32]{1,0:T(8,128)S(1)}, s32[32,32]{1,0:T(8,128)S(1)}, u32[]{:S(2)}, u32[]{:S(2)}) collective-permute-start(s32[32,32]{1,0:T(8,128)S(1)} %get-tuple-element.47), channel_id=1, source_target_pairs={{0,2},{1,3},{2,0},{3,1},{4,6},{5,7},{6,4},{7,5},{8,10},{9,11},{10,... | collective-permute-start | bytes 12296 | tf_op jit(solution)/shard_map/ppermute | solution.py:540
  48.6 3.0 %collective-permute-start.2 = (s32[32,32]{1,0:T(8,128)S(1)}, s32[32,32]{1,0:T(8,128)S(1)}, u32[]{:S(2)}, u32[]{:S(2)}) collective-permute-start(s32[32,32]{1,0:T(8,128)S(1)} %get-tuple-element.47), channel_id=1, source_target_pairs={{0,3},{1,0},{2,1},{3,2},{4,7},{5,4},{6,5},{7,6},{8,11},{9,8},{10,9... | collective-permute-start | bytes 12296 | tf_op jit(solution)/shard_map/ppermute | solution.py:540
  93.1 41.5 %all-to-all-start.2 = ((bf16[128,32,256]{2,1,0:T(8,128)(2,1)}), bf16[128,32,256]{2,1,0:T(8,128)(2,1)S(1)}, u32[]{:S(2)}, u32[]{:S(2)}) async-start(bf16[128,32,256]{2,1,0:T(8,128)(2,1)} %bitcast.28), calls=%async_computation.2 | async-start | bytes 4194304 | tf_op jit(solution)/shard_map/all_to_all | solution.py:553
  134.6 36.5 %copy-start = (bf16[128,32,256]{2,1,0:T(8,128)(2,1)}, bf16[128,32,256]{2,1,0:T(8,128)(2,1)S(1)}, u32[]{:S(2)}) copy-start(bf16[128,32,256]{2,1,0:T(8,128)(2,1)S(1)} %all-to-all-done.2) | copy-start | bytes 6291460
  171.1 29.2 %all-to-all-start.4 = ((bf16[128,48,128]{2,1,0:T(8,128)(2,1)}), bf16[128,48,128]{2,1,0:T(8,128)(2,1)S(1)}, u32[]{:S(2)}, u32[]{:S(2)}) async-start(bf16[128,48,128]{2,1,0:T(8,128)(2,1)} %total_parts.1), calls=%async_computation.4 | async-start | bytes 3145728 | tf_op jit(solution)/shard_map/all_to_all | solution.py:562

commit v4 on v3

--- a/solution.py
+++ b/solution.py
@@ -46,12 +46,31 @@
     lax.fori_loop(0, count // step, body, 0)
 
 
+def merged(table, spots):
+    sublane = lax.broadcasted_iota(jnp.int32, (8, 128), 0) // 2
+    found = [table[pl.ds(spot + (8 - 2 * k), 8), :] for k, spot in enumerate(spots)]
+    lower = jnp.where(sublane == 0, found[0], found[1])
+    upper = jnp.where(sublane == 2, found[2], found[3])
+    return jnp.where(sublane < 2, lower, upper)
+
+
+def pick_pairs(index_ref, offset, table, stage, count, low, high):
+    for r in range(0, count, 4):
+        words = [index_ref[offset + r + k] for k in range(4)]
+        stage[2 * (low + r) : 2 * (low + r) + 8, :] = merged(table, [word & 0xFFFF for word in words])
+        stage[2 * (high + r) : 2 * (high + r) + 8, :] = merged(table, [word >> 16 for word in words])
+
+
 def pick_rows(index_ref, offset, table, stage, count, start=0):
     for r in range(start, start + count):
         spot = index_ref[offset + r]
         stage[2 * r : 2 * r + 2, :] = table[pl.ds(pl.multiple_of(spot, 2), 2), :]
 
 
+def paired(first, second):
+    return (2 * first) | (second << 17)
+
+
 def joined(stage, start, count):
     left = stage[pl.ds(2 * start, count, stride=2), :]
     right = stage[pl.ds(2 * start + 1, count, stride=2), :]
@@ -62,14 +81,17 @@
     block = pl.program_id(0)
     step = stage.shape[0] // 2
     count = out_ref.shape[0]
+    half = 128
 
     @pl.when(block == 0)
     def _():
-        spread_table(rows_ref, table, 0, 256)
+        spread_table(rows_ref, table, 8, 256)
 
     def body(i, carry):
         base = pl.multiple_of(i * step, step)
-        pick_rows(index_ref, block * count + base, table, stage, step)
+        for k in range(step // (2 * half)):
+            word = (block * count + base) // 2 + k * half
+            pick_pairs(index_ref, word, table, stage, half, 2 * k * half, (2 * k + 1) * half)
         out_ref[pl.ds(base, step), :] = joined(stage, 0, step).astype(BF16)
         return carry
 
@@ -77,7 +99,7 @@
 
 
 def serve(index, memory):
-    count = index.shape[0]
+    count = 2 * index.shape[0]
     rows, width = memory.shape
     blocks = 4
     return pl.pallas_call(
@@ -86,7 +108,7 @@
         grid=(blocks,),
         in_specs=[SMEM, VMEM],
         out_specs=pl.BlockSpec((count // blocks, width), lambda i: (i, 0)),
-        scratch_shapes=[pltpu.VMEM((2 * rows, 128), F32), pltpu.VMEM((256, 128), F32)],
+        scratch_shapes=[pltpu.VMEM((2 * rows + 16, 128), F32), pltpu.VMEM((2048, 128), F32)],
         compiler_params=pltpu.CompilerParams(vmem_limit_bytes=LIMIT),
         cost_estimate=cost(11),
         name="serve_rows",
@@ -110,17 +132,16 @@
 
 
 def memory_kernel(
-    src_ref, dst_ref, src_row_ref, rows_ref, w_input_ref, w_hidden_ref,
+    pair_ref, src_row_ref, rows_ref, w_input_ref, w_hidden_ref,
     mem_src_ref, mem_dst_ref, change_ref, table, stage, delta,
 ):
-    spread_table(rows_ref, table, 0, 256)
+    spread_table(rows_ref, table, 8, 256)
     step = stage.shape[0] // 4
     events = mem_src_ref.shape[0]
 
     def body(i, carry):
         base = pl.multiple_of(i * step, step)
-        pick_rows(src_ref, base, table, stage, step)
-        pick_rows(dst_ref, base, table, stage.at[pl.ds(2 * step, 2 * step)], step)
+        pick_pairs(pair_ref, base, table, stage, step, 0, step)
         mem_src = joined(stage, 0, step).astype(BF16)
         mem_dst = joined(stage, step, step).astype(BF16)
         mem_src_ref[pl.ds(base, step), :] = mem_src
@@ -154,17 +175,17 @@
             jax.ShapeDtypeStruct((events, width), BF16),
             jax.ShapeDtypeStruct((owners, reps, UCAP, width), BF16),
         ),
-        in_specs=[SMEM, SMEM, VMEM, VMEM, VMEM, VMEM],
+        in_specs=[SMEM, VMEM, VMEM, VMEM, VMEM],
         out_specs=(VMEM, VMEM, VMEM),
         scratch_shapes=[
-            pltpu.VMEM((2 * count, 128), F32),
-            pltpu.VMEM((512, 128), F32),
+            pltpu.VMEM((2 * count + 16, 128), F32),
+            pltpu.VMEM((1024, 128), F32),
             pltpu.VMEM((events, width), BF16),
         ],
         compiler_params=pltpu.CompilerParams(vmem_limit_bytes=LIMIT),
         cost_estimate=cost(8),
         name="memory_step",
-    )(2 * src_slot, 2 * dst_slot, src_slot.reshape(1, events), fetched, w_input, w_hidden)
+    )(paired(src_slot, dst_slot), src_slot.reshape(1, events), fetched, w_input, w_hidden)
 
 
 COS_TERMS = (
@@ -225,20 +246,29 @@
     )(spacing, frequency.reshape(freqs, 1), w_time)
 
 
+def pick_quads(index_ref, offset, table, stage, count, start=0):
+    for r in range(start, start + count, 4):
+        stage[2 * r : 2 * r + 8, :] = merged(table, [index_ref[offset + r + k] for k in range(4)])
+
+
+def twice(x):
+    return jnp.concatenate([x, x], axis=1)
+
+
 def events_kernel(
     nbr_ref, rows_ref, phase_ref, timed_ref, mem_src_ref, mem_dst_ref, slope_ref,
     w_input_ref, w_hidden_ref, w_time_ref, w_query_ref, w_key_ref, w_value_ref, w_out_ref,
     grads_ref,
     rows_in, phase, timed, table, stage, ones, mixed, keys, values, score, dprob, slopes,
     hidden_half, query, dattended, reset, update, candidate, hid_c, attended, dquery,
-    acc_time, acc_kv, both_weights, dmixed, row_sems, time_sems, phase_sem,
+    acc_time, acc_kv, both_weights, query_weights, out_weights, order, row_sems, time_sems, phase_sem,
 ):
     events, width = slope_ref.shape
     nbrs = nbr_ref.shape[0] // events
     flat = stage.shape[0] // 2
     size = flat // nbrs
     blocks = events // size
-    large = dmixed.shape[0]
+    large = 2560
     head = width // HEADS
     scale = head ** -0.5
     chunks = row_sems.shape[0]
@@ -261,11 +291,19 @@
         time_copy(c).start()
     phase_copy = pltpu.make_async_copy(phase_ref, phase, phase_sem)
     phase_copy.start()
-    row_id = lax.broadcasted_iota(jnp.int32, (width, width), 0) // head
-    col_id = lax.broadcasted_iota(jnp.int32, (width, width), 1) // head
-    ones[...] = jnp.where(row_id == col_id, 1.0, 0.0).astype(BF16)
-    both_weights[:, :width] = w_key_ref[...]
-    both_weights[:, width:] = w_value_ref[...]
+    old_column = lax.broadcasted_iota(jnp.int32, (width, width), 0)
+    new_column = lax.broadcasted_iota(jnp.int32, (width, width), 1)
+    lanes = width // 2
+    part_head = head // 2
+    moved = (new_column % lanes) // part_head * head + new_column // lanes * part_head + new_column % part_head
+    order[...] = jnp.where(moved == old_column, 1.0, 0.0).astype(BF16)
+    of_row = lax.broadcasted_iota(jnp.int32, (width, lanes), 0) % lanes // part_head
+    of_lane = lax.broadcasted_iota(jnp.int32, (width, lanes), 1) // part_head
+    ones[...] = jnp.where(of_row == of_lane, 1.0, 0.0).astype(BF16)
+    query_weights[...] = dot(w_query_ref[...], order[...]).astype(BF16)
+    out_weights[...] = dot_tn(order[...], w_out_ref[...]).astype(BF16)
+    both_weights[:, :width] = dot(w_key_ref[...], order[...]).astype(BF16)
+    both_weights[:, width:] = dot(w_value_ref[...], order[...]).astype(BF16)
     for ref in (acc_time, acc_kv):
         ref[...] = jnp.zeros_like(ref)
 
@@ -278,15 +316,15 @@
         hid_c[span, :] = h
         half = hidden.astype(BF16)
         hidden_half[span, :] = half
-        query[span, :] = dot(half, w_query_ref[...]).astype(BF16)
-        dattended[span, :] = dot_nt(slope_ref[span, :], w_out_ref[...]).astype(BF16)
+        query[span, :] = dot(half, query_weights[...]).astype(BF16)
+        dattended[span, :] = dot_nt(slope_ref[span, :], out_weights[...]).astype(BF16)
         return carry
 
     lax.fori_loop(0, events // 256, forward, 0)
     for c in range(chunks):
         row_copies[c].wait()
-        spread_table(rows_in.at[pl.ds(c * part, part)], table, 2 * c * part, 256)
-    pick_rows(nbr_ref, 0, table, stage, flat)
+        spread_table(rows_in.at[pl.ds(c * part, part)], table, 8 + 2 * c * part, 256)
+    pick_quads(nbr_ref, 0, table, stage, flat)
     def body(i, carry):
         at = pl.multiple_of(i * flat, flat)
         event = pl.multiple_of(i * size, size)
@@ -298,8 +336,8 @@
 
         rows = (joined(stage, 0, flat) + timed[pl.ds(at, flat), :].astype(F32)).astype(BF16)
         mixed[pl.ds(at, flat), :] = rows
-        key = dot(rows, w_key_ref[...]).astype(BF16)
-        value = dot(rows, w_value_ref[...]).astype(BF16)
+        key = dot(rows, both_weights[:, :width]).astype(BF16)
+        value = dot(rows, both_weights[:, width:]).astype(BF16)
         keys[...] = key
         values[...] = value
         key_side, value_side = [], []
@@ -321,25 +359,25 @@
             weights = [jnp.exp2((s - top) * (scale * math.log2(math.e))) for s in scores]
             total = functools.reduce(jnp.add, weights)
             inverse = 1.0 / total
-            outcome, overlap = jnp.zeros_like(top), jnp.zeros_like(top)
+            outcome, overlap = jnp.zeros((GROUP, width), F32), jnp.zeros_like(top)
             for j in range(nbrs):
-                outcome = outcome + weights[j] * values[spans[j], :].astype(F32)
+                outcome = outcome + twice(weights[j]) * values[spans[j], :].astype(F32)
                 overlap = overlap + weights[j] * dprob[spans[j], :]
-                pick_rows(nbr_ref, upcoming, table, stage, GROUP // 2, (g * nbrs + j) * GROUP)
+                pick_quads(nbr_ref, upcoming, table, stage, GROUP // 2, (g * nbrs + j) * GROUP)
             overlap = overlap * inverse
-            attended[own, :] = (outcome * inverse).astype(BF16)
+            attended[own, :] = (outcome * twice(inverse)).astype(BF16)
             datt = dattended[own, :].astype(F32)
             asked = query[own, :].astype(F32) * scale
-            change = jnp.zeros_like(top)
+            change = jnp.zeros((GROUP, width), F32)
             for j in range(nbrs):
                 span = spans[j]
                 prob = weights[j] * inverse
-                dscore = prob * (dprob[span, :] - overlap)
+                dscore = twice(prob * (dprob[span, :] - overlap))
                 change = change + dscore * keys[span, :].astype(F32)
                 here = pl.ds(at + (g * nbrs + j) * GROUP, GROUP)
                 slopes[here, :width] = (dscore * asked).astype(BF16)
-                slopes[here, width:] = (prob * datt).astype(BF16)
-                pick_rows(nbr_ref, upcoming, table, stage, GROUP // 2, (g * nbrs + j) * GROUP + GROUP // 2)
+                slopes[here, width:] = (twice(prob) * datt).astype(BF16)
+                pick_quads(nbr_ref, upcoming, table, stage, GROUP // 2, (g * nbrs + j) * GROUP + GROUP // 2)
             dquery[own, :] = (change * scale).astype(BF16)
         return carry
 
@@ -347,24 +385,22 @@
 
     phase_copy.wait()
     for i in range(nbrs * events // large):
-        for k in range(large // 256):
-            span = slice(i * large + k * 256, i * large + (k + 1) * 256)
-            dmixed[k * 256 : (k + 1) * 256, :] = dot_nt(slopes[span, :], both_weights[...]).astype(BF16)
         span = slice(i * large, (i + 1) * large)
-        acc_time[...] += dot(phase[:, span], dmixed[...])
+        acc_time[...] += dot(phase[:, span], slopes[span, :])
         acc_kv[...] += dot_tn(mixed[span, :], slopes[span, :])
     total_rows = 0
+    packed_ref = grads_ref
 
     def write(value):
         nonlocal total_rows
         depth, columns = value.shape
         for k in range(columns // 128):
-            grads_ref[total_rows : total_rows + depth, :] = value[:, k * 128 : (k + 1) * 128].astype(BF16)
+            packed_ref[total_rows : total_rows + depth, :] = value[:, k * 128 : (k + 1) * 128].astype(BF16)
             total_rows += depth
 
     mem_src, mem_dst, slope = mem_src_ref[...], mem_dst_ref[...], slope_ref[...]
     rows = mem_src.astype(F32)
-    dhidden = slope.astype(F32) + dot_nt(dquery[...], w_query_ref[...])
+    dhidden = slope.astype(F32) + dot_nt(dquery[...], query_weights[...])
     u, c, r = update[...], candidate[...], reset[...]
     dcand = dhidden * (1.0 - u) * (1.0 - c * c)
     dupdate = (dhidden * (rows - c) * u * (1.0 - u)).astype(BF16)
@@ -373,15 +409,16 @@
         write(dot_tn(mem_dst, piece))
     for piece in (dreset, dupdate, (dcand * r).astype(BF16)):
         write(dot_tn(mem_src, piece))
-    write(acc_time[...])
-    write(dot_tn(hidden_half[...], dquery[...]))
-    write(acc_kv[...])
-    write(dot_tn(attended[...], slope))
-    if total_rows < grads_ref.shape[0]:
-        grads_ref[total_rows:, :] = jnp.zeros((grads_ref.shape[0] - total_rows, 128), BF16)
-
-
-def events_step(nbr_index, fetched, phase, timed, mem_src, mem_dst, slope, weights, grad_rows, size=64):
+    time_high = acc_time[...].astype(BF16)
+    time_low = (acc_time[...] - time_high.astype(F32)).astype(BF16)
+    write(dot_nt(time_high, both_weights[...]) + dot_nt(time_low, both_weights[...]))
+    write(dot_nt(dot_tn(hidden_half[...], dquery[...]).astype(BF16), order[...]))
+    write(dot_nt(acc_kv[:, :width].astype(BF16), order[...]))
+    write(dot_nt(acc_kv[:, width:].astype(BF16), order[...]))
+    write(dot(order[...], dot_tn(attended[...], slope).astype(BF16)))
+
+
+def events_step(nbr_index, fetched, phase, timed, mem_src, mem_dst, slope, weights, grad_rows, size=128):
     events, width = slope.shape
     nbrs = nbr_index.shape[0] // events
     count = fetched.shape[0]
@@ -399,25 +436,27 @@
             pltpu.VMEM((count, width), BF16),
             pltpu.VMEM((freqs, nbrs * events), BF16),
             pltpu.VMEM((nbrs * events, width), BF16),
-            pltpu.VMEM((2 * count, 128), F32),
+            pltpu.VMEM((2 * count + 16, 128), F32),
             pltpu.VMEM((2 * flat, 128), F32),
-            pltpu.VMEM((width, width), BF16),
+            pltpu.VMEM((width, width // 2), BF16),
             pltpu.VMEM((nbrs * events, width), BF16),
             pltpu.VMEM((flat, width), BF16),
             pltpu.VMEM((flat, width), BF16),
-            pltpu.VMEM((flat, width), F32),
-            pltpu.VMEM((flat, width), F32),
+            pltpu.VMEM((flat, width // 2), F32),
+            pltpu.VMEM((flat, width // 2), F32),
             pltpu.VMEM((nbrs * events, 2 * width), BF16),
             halves, halves, halves, wholes, wholes, wholes, wholes, halves, halves,
-            pltpu.VMEM((freqs, width), F32),
+            pltpu.VMEM((freqs, 2 * width), F32),
             pltpu.VMEM((width, 2 * width), F32),
             pltpu.VMEM((width, 2 * width), BF16),
-            pltpu.VMEM((2560, width), BF16),
+            pltpu.VMEM((width, width), BF16),
+            pltpu.VMEM((width, width), BF16),
+            pltpu.VMEM((width, width), BF16),
             pltpu.SemaphoreType.DMA((8,)),
             pltpu.SemaphoreType.DMA((4,)),
             pltpu.SemaphoreType.DMA,
         ],
-        compiler_params=pltpu.CompilerParams(vmem_limit_bytes=LIMIT),
+        compiler_params=pltpu.CompilerParams(vmem_limit_bytes=54 * 1024 * 1024),
         cost_estimate=cost(40),
         name="events_step",
     )(nbr_index, fetched, phase, timed, mem_src, mem_dst, slope, *weights)
@@ -475,28 +514,41 @@
     )(place, index, change, memory)
 
 
-def total_kernel(parts_ref, out_ref):
-    total = jnp.zeros(parts_ref.shape[1:], F32)
-    for k in range(parts_ref.shape[0]):
-        total = total + parts_ref[k].astype(F32)
-    total = total.astype(BF16)
-    for k in range(parts_ref.shape[0]):
-        out_ref[k] = total
-
-
-def total_parts(parts):
+TILE = 8
+
+
+def total_kernel(parts_ref, out_ref, spread):
+    share = spread.shape[0] // TILE
+    parts, out = parts_ref, out_ref
+    group = spread.shape[0]
+    total = jnp.zeros((group, 128), F32)
+    for k in range(parts.shape[0] // group):
+        total = total + parts[k * group : (k + 1) * group, :].astype(F32)
+    one = total[:share]
+    for k in range(1, TILE):
+        one = one + total[k * share : (k + 1) * share]
+    for k in range(TILE):
+        spread[k * share : (k + 1) * share, :] = one
+    whole = spread[...].astype(BF16)
+    for k in range(parts.shape[0] // group):
+        out[k * group : (k + 1) * group, :] = whole
+
+
+def total_parts(parts, share):
     return pl.pallas_call(
         total_kernel,
         out_shape=jax.ShapeDtypeStruct(parts.shape, BF16),
         in_specs=[VMEM],
         out_specs=VMEM,
+        scratch_shapes=[pltpu.VMEM((TILE * share, 128), F32)],
         compiler_params=pltpu.CompilerParams(vmem_limit_bytes=8 * 1024 * 1024),
         cost_estimate=cost(3),
         name="total_parts",
     )(parts)
 
 
-def unpack_kernel(flat_ref, *out_refs):
+def unpack_kernel(packed_ref, *out_refs):
+    flat_ref = packed_ref
     row = 0
     for out_ref in out_refs:
         depth, columns = out_ref.shape
@@ -520,6 +572,12 @@
 BOTH = ("node", "rep")
 
 
+def exchange(rows):
+    pairs = lax.optimization_barrier(rows.reshape(rows.shape[0] // 2, 2, 128))
+    pairs = lax.all_to_all(pairs, BOTH, split_axis=0, concat_axis=0, tiled=True)
+    return lax.optimization_barrier(pairs).reshape(rows.shape)
+
+
 def local(
     memory, req_rows, src_slot, dst_slot, nbr_slot, event_time, nbr_time, frequency, emb_grad,
     w_input, w_hidden, w_time, w_query, w_key, w_value, w_out,
@@ -529,13 +587,14 @@
     owners, capacity = requests.shape
     width = memory.shape[1]
     reps = lax.axis_size("rep")
-    doubled = lax.optimization_barrier((2 * requests).reshape(owners, capacity // 128, 128))
-    asked = lax.all_to_all(doubled, "node", split_axis=0, concat_axis=0, tiled=True)
-    asked = asked.reshape(owners, capacity)
+    half = capacity // 2
+    words = lax.optimization_barrier(paired(requests[:, :half], requests[:, half:]).reshape(owners, 1, half))
+    asked = lax.all_to_all(words, "node", split_axis=0, concat_axis=0, tiled=True)
+    asked = asked.reshape(owners, half)
     served = serve(asked.reshape(-1), memory).reshape(owners, capacity, width)
     fetched = lax.all_to_all(served, "node", split_axis=0, concat_axis=0, tiled=True)
     fetched = fetched.reshape(owners * capacity, width)
-    lead = asked[:, :UCAP]
+    lead = asked[:, :UCAP] & 0xFFFF
     turned = [lead] + [
         lax.ppermute(lead, "rep", [(i, (i + k) % reps) for i in range(reps)]) for k in range(1, reps)
     ]
@@ -554,12 +613,12 @@
     shapes = (w_input.shape, w_hidden.shape, w_time.shape, w_query.shape, w_key.shape, w_value.shape, w_out.shape)
     used = sum(shape[0] * shape[1] for shape in shapes) // 128
     devices = owners * reps
-    share = -(-used // (devices * 16)) * 16
+    share = used // devices
     grads = events_step(nbr_index, fetched, phase, timed, mem_src, mem_dst, emb_grad, weights, devices * share)
     grads, updates = lax.optimization_barrier((grads, updates))
-    parts = lax.all_to_all(grads, BOTH, split_axis=0, concat_axis=0, tiled=True)
-    summed = total_parts(parts.reshape(devices, share, 128))
-    flat = lax.all_to_all(summed.reshape(devices * share, 128), BOTH, split_axis=0, concat_axis=0, tiled=True)
+    parts = exchange(grads)
+    summed = total_parts(parts, share)
+    flat = exchange(summed)
     new_memory = merge(place, touched, updates, memory)
     return (new_memory, *unpack(flat, shapes))
 

time: 203 us -> 194 us (0.956)
  Pallas kernels: 76.7 us -> 72.1 us
  blocking collectives: 51.6 us -> 48.7 us
    pallas_call x1, Pallas kernels: 33.6 us -> 30.2 us  [events_step(): pl.pallas_call(events_kernel, out_shape=jax.ShapeDtypeStruct((grad_rows,...]
    all_to_all x2, blocking collectives: 51.6 us -> 48.7 us  [the longest x1 32.2 us: exchange(): pairs = lax.all_to_all(pairs, BOTH, split_axis=0, concat_axis=0, tiled=True)]
    all_to_all x1, waiting for transfers between devices: 13.9 us -> 11.7 us  [exchange(): pairs = lax.all_to_all(pairs, BOTH, split_axis=0, concat_axis=0, tiled=True)]
  transfers between devices with their start and end apart: 6 -> 6, of which waited for: 3 -> 5; matrix products, arithmetic and copies ran while one was open for 2% -> 2% of each run, Pallas kernels for 27% -> 26%
where the time goes in v4:
time: 194 us; the launch traced here: 193 us
  Pallas kernels  72.1 us (37%)
  blocking collectives  48.7 us (25%)
  waiting for transfers between devices  45.1 us (23%)
  starting transfers between devices  21.1 us (11%)
  local copies, waits for them, and re-layouts  3.69 us (2%)
    all_to_all x1, blocking collectives, exchange(): pairs = lax.all_to_all(pairs, BOTH, split_axis=0, concat_axis=0, tiled=True)  32.2 us
    all_to_all x1, waiting for transfers between devices, local(): lax.all_to_all(served, 'node', split_axis=0, concat_axis=0, tiled=True)  31.6 us
    pallas_call x1, Pallas kernels, events_step(): pl.pallas_call(events_kernel, out_shape=jax.ShapeDtypeStruct((grad_rows,...  30.2 us
    all_to_all x1, blocking collectives, local(): lax.all_to_all(words, 'node', split_axis=0, concat_axis=0, tiled=True)  16.5 us
    all_to_all x1, waiting for transfers between devices, exchange(): pairs = lax.all_to_all(pairs, BOTH, split_axis=0, concat_axis=0, tiled=True)  11.7 us
    pallas_call x1, Pallas kernels, merge(): pl.pallas_call(merge_kernel, out_shape=jax.ShapeDtypeStruct((rows, width)...  11.5 us
    pallas_call x1, Pallas kernels, serve(): pl.pallas_call(serve_kernel, out_shape=jax.ShapeDtypeStruct((count, width...  10 us
    pallas_call x1, Pallas kernels, phase_step(): pl.pallas_call(phase_kernel, out_shape=(jax.ShapeDtypeStruct((freqs, tota...  8.97 us
  transfers between devices with their start and end apart: 6, of which 5 were waited for; matrix products, arithmetic and copies ran while one was open for 2% of the time, Pallas kernels for 26%

profile of v4, /device:TPU:1, one launch (start us, length us, event | category | flops | bytes accessed | tf_op | source)
XLA Modules:
  0.0 192.9 jit_solution(8888665898027482534)
XLA Ops:
  0.6 0.7 fusion
  1.4 16.5 %all_to_all.32 = s32[32,1,128]{2,1,0:T(1,128)} all-to-all(s32[32,1,128]{2,1,0:T(1,128)S(1)} %bitcast.36), channel_id=1, replica_groups=mesh['node'=32,'rep'=4] {'node'}, dimensions={0} | all-to-all | bytes 32768 | tf_op jit(solution)/shard_map/all_to_all | solution.py:592
  17.8 10.0 %serve_rows.1 = bf16[8192,256]{1,0:T(8,128)(2,1)} custom-call(s32[4096]{0:T(1024)} %bitcast.34, bf16[4096,256]{1,0:T(8,128)(2,1)} %memory_ref.1), custom_call_target="tpu_custom_call" | custom-call | flops 12099999744 | bytes 33000000 | tf_op jit(solution)/shard_map/serve_rows/pallas_call | solution.py:105
  27.9 5.0 %all-to-all-start.1 = ((bf16[32,256,256]{2,1,0:T(8,128)(2,1)}), bf16[32,256,256]{2,1,0:T(8,128)(2,1)}, u32[]{:S(2)}, u32[]{:S(2)}) async-start(bf16[32,256,256]{2,1,0:T(8,128)(2,1)} %bitcast.28), calls=%async_computation.1 | async-start | bytes 8388608 | tf_op jit(solution)/shard_map/all_to_all | solution.py:595
  33.0 0.1 reshape.77
  33.1 0.2 copy.30
  33.4 0.8 reshape.78.spacing_ref
  34.1 0.7 copy.31.freq_ref
  34.9 0.0 copy-start.5
  34.9 0.0 copy-start.6
  34.9 9.0 %phase_step.1 = (bf16[128,10240]{1,0:T(8,128)(2,1)}, bf16[10240,256]{1,0:T(8,128)(2,1)}) custom-call(f32[1,10240]{1,0:T(1,128)} %reshape.78.spacing_ref, f32[128,1]{1,0:T(8,128)} %copy.31.freq_ref, bf16[128,256]{1,0:T(8,128)(2,1)} %w_time_ref.3), custom_call_target="tpu_custom_call" | custom-call | flops 11000000512 | bytes 30000000 | tf_op jit(solution)/shard_map/phase_step/pallas_call | solution.py:227
  43.9 2.5 %collective-permute-start.2 = (s32[32,32]{1,0:T(8,128)S(1)}, s32[32,32]{1,0:T(8,128)S(1)}, u32[]{:S(2)}, u32[]{:S(2)}) collective-permute-start(s32[32,32]{1,0:T(8,128)S(1)} %get-tuple-element.47), channel_id=1, source_target_pairs={{0,3},{1,0},{2,1},{3,2},{4,7},{5,4},{6,5},{7,6},{8,11},{9,8},{10,9... | collective-permute-start | bytes 12296 | tf_op jit(solution)/shard_map/ppermute | solution.py:599
  46.5 0.0 collective-permute-start
  46.5 1.7 collective-permute-start.1
  48.2 0.6 shift-left_or_fusion.pair_ref
  48.8 0.1 reshape.75
  48.9 0.2 copy.29
  49.1 0.8 reshape.76.nbr_ref
  49.9 0.8 collective-permute-done
  50.7 0.4 collective-permute-done.1
  51.0 0.7 reshape.74.index_ref
  51.7 31.6 %all-to-all-done.1 = bf16[32,256,256]{2,1,0:T(8,128)(2,1)} async-done(((bf16[32,256,256]{2,1,0:T(8,128)(2,1)}), bf16[32,256,256]{2,1,0:T(8,128)(2,1)}, u32[]{:S(2)}, u32[]{:S(2)}) %all-to-all-start.1) | async-done | bytes 4194336 | tf_op jit(solution)/shard_map/all_to_all | solution.py:595
  83.3 8.5 %memory_step.1 = (bf16[1024,256]{1,0:T(8,128)(2,1)}, bf16[1024,256]{1,0:T(8,128)(2,1)}, bf16[32,4,32,256]{3,2,1,0:T(8,128)(2,1)}) custom-call(s32[1024]{0:T(1024)} %shift-left_or_fusion.pair_ref, s32[1,1024]{1,0:T(1,128)} %bitcast.41, bf16[8192,256]{1,0:T(8,128)(2,1)} %bitcast.5.rows_ref, bf16[256,768]{1,0:T(8,128)(2,1)} %w_input_ref.3, ...), custom_call_target="tpu_custom_call" | custom-call | flops 8800000000 | bytes 24000000 | tf_op jit(solution)/shard_map/memory_step/pallas_call | solution.py:171
  91.8 7.9 %all-to-all-start.2 = ((bf16[128,32,256]{2,1,0:T(8,128)(2,1)}), bf16[128,32,256]{2,1,0:T(8,128)(2,1)S(1)}, u32[]{:S(2)}, u32[]{:S(2)}) async-start(bf16[128,32,256]{2,1,0:T(8,128)(2,1)} %bitcast.30), calls=%async_computation.2 | async-start | bytes 4194304 | tf_op jit(solution)/shard_map/all_to_all | solution.py:612
  99.8 30.2 %events_step.1 = bf16[5376,128]{1,0:T(8,128)(2,1)} custom-call(s32[10240]{0:T(1024)} %reshape.76.nbr_ref, bf16[8192,256]{1,0:T(8,128)(2,1)} %bitcast.5.rows_ref, bf16[128,10240]{1,0:T(8,128)(2,1)} %get-tuple-element.32.phase_ref, bf16[10240,256]{1,0:T(8,128)(2,1)} %get-tuple-element.33.timed_ref, bf16[1024,256]{1,0:T(8,128)(2,1)} %get-tuple-element.34.mem_src_ref, ...), custom_call_target="tpu_custom_call" | custom-call | flops 44000002048 | bytes 120000000 | tf_op jit(solution)/shard_map/events_step/pallas_call | solution.py:430
  129.9 0.7 all-to-all-done.2
  130.6 32.2 %all_to_all.33 = bf16[2688,2,128]{2,1,0:T(2,128)(2,1)S(1)} all-to-all(bf16[2688,2,128]{2,1,0:T(2,128)(2,1)} %bitcast.31), channel_id=1, replica_groups=mesh['node'=32,'rep'=4] {'node','rep'}, dimensions={0} | all-to-all | bytes 2752512 | tf_op jit(solution)/shard_map/all_to_all | solution.py:577
  162.8 1.4 total_parts.1
  164.2 3.8 %all-to-all-start.4 = ((bf16[2688,2,128]{2,1,0:T(2,128)(2,1)}), bf16[2688,2,128]{2,1,0:T(2,128)(2,1)S(1)}, u32[]{:S(2)}, u32[]{:S(2)}) async-start(bf16[2688,2,128]{2,1,0:T(2,128)(2,1)} %bitcast.19), calls=%async_computation.4 | async-start | bytes 2752512 | tf_op jit(solution)/shard_map/all_to_all | solution.py:577
  168.1 11.5 %merge_rows.1 = bf16[4096,256]{1,0:T(8,128)(2,1)} custom-call(s32[1]{0:T(128)} %bitcast.place_ref, s32[4096]{0:T(1024)} %reshape.74.index_ref, bf16[4096,256]{1,0:T(8,128)(2,1)} %bitcast.29, bf16[4096,256]{1,0:T(8,128)(2,1)} %memory_ref.1), custom_call_target="tpu_custom_call" | custom-call | flops 12099999744 | bytes 33000000 | tf_op jit(solution)/shard_map/merge_rows/pallas_call | solution.py:505
  179.6 11.7 %all-to-all-done.4 = bf16[2688,2,128]{2,1,0:T(2,128)(2,1)S(1)} async-done(((bf16[2688,2,128]{2,1,0:T(2,128)(2,1)}), bf16[2688,2,128]{2,1,0:T(2,128)(2,1)S(1)}, u32[]{:S(2)}, u32[]{:S(2)}) %all-to-all-start.4) | async-done | bytes 1376288 | tf_op jit(solution)/shard_map/all_to_all | solution.py:577
  191.3 1.6 unpack_grads.1
  (19 shorter events, 0.1 us)
Async XLA Ops:
  27.9 5.1 %copy-start.2 = (s32[1024,10]{0,1:T(8,128)S(1)}, s32[1024,10]{0,1:T(8,128)}, u32[]{:S(2)}) copy-start(s32[1024,10]{0,1:T(8,128)} %param.22) | copy-start | bytes 122884
  27.9 5.1 %copy-start.4 = (s32[1024]{0:T(1024)S(1)}, s32[1024]{0:T(1024)}, u32[]{:S(2)}) copy-start(s32[1024]{0:T(1024)} %param.21) | copy-start | bytes 12292
  27.9 6.2 %copy-start.7 = (f32[128]{0:T(128)S(1)}, f32[128]{0:T(128)}, u32[]{:S(2)}) copy-start(f32[128]{0:T(128)} %param.23) | copy-start | bytes 1540
  27.9 7.0 %copy-start.3 = (s32[1024,10]{0,1:T(8,128)S(1)}, s32[1024,10]{0,1:T(8,128)}, u32[]{:S(2)}) copy-start(s32[1024,10]{0,1:T(8,128)} %param.20) | copy-start | bytes 122884
  27.9 55.4 %all-to-all-start.1 = ((bf16[32,256,256]{2,1,0:T(8,128)(2,1)}), bf16[32,256,256]{2,1,0:T(8,128)(2,1)}, u32[]{:S(2)}, u32[]{:S(2)}) async-start(bf16[32,256,256]{2,1,0:T(8,128)(2,1)} %bitcast.28), calls=%async_computation.1 | async-start | bytes 8388608 | tf_op jit(solution)/shard_map/all_to_all | solution.py:595
  34.9 9.0 %copy-start.1 = (s32[32,1,128]{2,1,0:T(1,128)S(1)}, s32[32,1,128]{2,1,0:T(1,128)}, u32[]{:S(2)}) copy-start(s32[32,1,128]{2,1,0:T(1,128)} %all_to_all.32) | copy-start | bytes 49156
  34.9 13.3 %copy-start.5 = (s32[1024]{0:T(1024)S(1)}, s32[1024]{0:T(1024)}, u32[]{:S(2)}) copy-start(s32[1024]{0:T(1024)} %param.19) | copy-start | bytes 12292
  34.9 13.3 %copy-start.6 = (s32[1024]{0:T(1024)S(1)}, s32[1024]{0:T(1024)}, u32[]{:S(2)}) copy-start(s32[1024]{0:T(1024)} %param.18) | copy-start | bytes 12292
  43.9 6.0 %collective-permute-start.2 = (s32[32,32]{1,0:T(8,128)S(1)}, s32[32,32]{1,0:T(8,128)S(1)}, u32[]{:S(2)}, u32[]{:S(2)}) collective-permute-start(s32[32,32]{1,0:T(8,128)S(1)} %get-tuple-element.47), channel_id=1, source_target_pairs={{0,3},{1,0},{2,1},{3,2},{4,7},{5,4},{6,5},{7,6},{8,11},{9,8},{10,9... | collective-permute-start | bytes 12296 | tf_op jit(solution)/shard_map/ppermute | solution.py:599
  46.5 4.2 %collective-permute-start = (s32[32,32]{1,0:T(8,128)S(1)}, s32[32,32]{1,0:T(8,128)S(1)}, u32[]{:S(2)}, u32[]{:S(2)}) collective-permute-start(s32[32,32]{1,0:T(8,128)S(1)} %get-tuple-element.47), channel_id=1, source_target_pairs={{0,1},{1,2},{2,3},{3,0},{4,5},{5,6},{6,7},{7,4},{8,9},{9,10},{10,1... | collective-permute-start | bytes 12296 | tf_op jit(solution)/shard_map/ppermute | solution.py:599
  46.5 4.6 %collective-permute-start.1 = (s32[32,32]{1,0:T(8,128)S(1)}, s32[32,32]{1,0:T(8,128)S(1)}, u32[]{:S(2)}, u32[]{:S(2)}) collective-permute-start(s32[32,32]{1,0:T(8,128)S(1)} %get-tuple-element.47), channel_id=1, source_target_pairs={{0,2},{1,3},{2,0},{3,1},{4,6},{5,7},{6,4},{7,5},{8,10},{9,11},{10,... | collective-permute-start | bytes 12296 | tf_op jit(solution)/shard_map/ppermute | solution.py:599
  91.8 38.8 %all-to-all-start.2 = ((bf16[128,32,256]{2,1,0:T(8,128)(2,1)}), bf16[128,32,256]{2,1,0:T(8,128)(2,1)S(1)}, u32[]{:S(2)}, u32[]{:S(2)}) async-start(bf16[128,32,256]{2,1,0:T(8,128)(2,1)} %bitcast.30), calls=%async_computation.2 | async-start | bytes 4194304 | tf_op jit(solution)/shard_map/all_to_all | solution.py:612
  130.6 33.7 %copy-start = (bf16[128,32,256]{2,1,0:T(8,128)(2,1)}, bf16[128,32,256]{2,1,0:T(8,128)(2,1)S(1)}, u32[]{:S(2)}) copy-start(bf16[128,32,256]{2,1,0:T(8,128)(2,1)S(1)} %all-to-all-done.2) | copy-start | bytes 6291460
  164.2 27.1 %all-to-all-start.4 = ((bf16[2688,2,128]{2,1,0:T(2,128)(2,1)}), bf16[2688,2,128]{2,1,0:T(2,128)(2,1)S(1)}, u32[]{:S(2)}, u32[]{:S(2)}) async-start(bf16[2688,2,128]{2,1,0:T(2,128)(2,1)} %bitcast.19), calls=%async_computation.4 | async-start | bytes 2752512 | tf_op jit(solution)/shard_map/all_to_all | solution.py:577

commit v5 on v4

--- a/solution.py
+++ b/solution.py
@@ -366,19 +366,19 @@
                 pick_quads(nbr_ref, upcoming, table, stage, GROUP // 2, (g * nbrs + j) * GROUP)
             overlap = overlap * inverse
             attended[own, :] = (outcome * twice(inverse)).astype(BF16)
-            datt = dattended[own, :].astype(F32)
-            asked = query[own, :].astype(F32) * scale
+            datt = dattended[own, :]
+            asked = query[own, :]
             change = jnp.zeros((GROUP, width), F32)
             for j in range(nbrs):
                 span = spans[j]
                 prob = weights[j] * inverse
-                dscore = twice(prob * (dprob[span, :] - overlap))
+                dscore = twice((prob * (dprob[span, :] - overlap)) * scale)
                 change = change + dscore * keys[span, :].astype(F32)
                 here = pl.ds(at + (g * nbrs + j) * GROUP, GROUP)
-                slopes[here, :width] = (dscore * asked).astype(BF16)
-                slopes[here, width:] = (twice(prob) * datt).astype(BF16)
+                slopes[here, :width] = dscore.astype(BF16) * asked
+                slopes[here, width:] = twice(prob.astype(BF16)) * datt
                 pick_quads(nbr_ref, upcoming, table, stage, GROUP // 2, (g * nbrs + j) * GROUP + GROUP // 2)
-            dquery[own, :] = (change * scale).astype(BF16)
+            dquery[own, :] = change.astype(BF16)
         return carry
 
     lax.fori_loop(0, blocks, body, 0)

time: 194 us -> 193 us (level)
  no operation moved by 1% of the time
where the time goes in v5:
time: 193 us; the launch traced here: 192 us
  Pallas kernels  71.7 us (37%)
  blocking collectives  48.3 us (25%)
  waiting for transfers between devices  45.6 us (24%)
  starting transfers between devices  21.1 us (11%)
  local copies, waits for them, and re-layouts  3.69 us (2%)
    all_to_all x1, blocking collectives, exchange(): pairs = lax.all_to_all(pairs, BOTH, split_axis=0, concat_axis=0, tiled=True)  31.8 us
    all_to_all x1, waiting for transfers between devices, local(): lax.all_to_all(served, 'node', split_axis=0, concat_axis=0, tiled=True)  31.6 us
    pallas_call x1, Pallas kernels, events_step(): pl.pallas_call(events_kernel, out_shape=jax.ShapeDtypeStruct((grad_rows,...  29.7 us
    all_to_all x1, blocking collectives, local(): lax.all_to_all(words, 'node', split_axis=0, concat_axis=0, tiled=True)  16.5 us
    all_to_all x1, waiting for transfers between devices, exchange(): pairs = lax.all_to_all(pairs, BOTH, split_axis=0, concat_axis=0, tiled=True)  11.7 us
    pallas_call x1, Pallas kernels, merge(): pl.pallas_call(merge_kernel, out_shape=jax.ShapeDtypeStruct((rows, width)...  11.5 us
    pallas_call x1, Pallas kernels, serve(): pl.pallas_call(serve_kernel, out_shape=jax.ShapeDtypeStruct((count, width...  10 us
    pallas_call x1, Pallas kernels, phase_step(): pl.pallas_call(phase_kernel, out_shape=(jax.ShapeDtypeStruct((freqs, tota...  8.97 us
  transfers between devices with their start and end apart: 6, of which 5 were waited for; matrix products, arithmetic and copies ran while one was open for 2% of the time, Pallas kernels for 26%

profile of v5, /device:TPU:1, one launch (start us, length us, event | category | flops | bytes accessed | tf_op | source)
XLA Modules:
  0.0 192.5 jit_solution(15685402776028632687)
XLA Ops:
  0.6 0.7 fusion
  1.4 16.5 %all_to_all.32 = s32[32,1,128]{2,1,0:T(1,128)} all-to-all(s32[32,1,128]{2,1,0:T(1,128)S(1)} %bitcast.36), channel_id=1, replica_groups=mesh['node'=32,'rep'=4] {'node'}, dimensions={0} | all-to-all | bytes 32768 | tf_op jit(solution)/shard_map/all_to_all | solution.py:592
  17.8 10.0 %serve_rows.1 = bf16[8192,256]{1,0:T(8,128)(2,1)} custom-call(s32[4096]{0:T(1024)} %bitcast.34, bf16[4096,256]{1,0:T(8,128)(2,1)} %memory_ref.1), custom_call_target="tpu_custom_call" | custom-call | flops 12099999744 | bytes 33000000 | tf_op jit(solution)/shard_map/serve_rows/pallas_call | solution.py:105
  27.9 5.1 %all-to-all-start.1 = ((bf16[32,256,256]{2,1,0:T(8,128)(2,1)}), bf16[32,256,256]{2,1,0:T(8,128)(2,1)}, u32[]{:S(2)}, u32[]{:S(2)}) async-start(bf16[32,256,256]{2,1,0:T(8,128)(2,1)} %bitcast.28), calls=%async_computation.1 | async-start | bytes 8388608 | tf_op jit(solution)/shard_map/all_to_all | solution.py:595
  33.0 0.1 reshape.77
  33.1 0.2 copy.30
  33.4 0.8 reshape.78.spacing_ref
  34.1 0.7 copy.31.freq_ref
  34.9 0.0 copy-start.5
  34.9 0.0 copy-start.6
  34.9 9.0 %phase_step.1 = (bf16[128,10240]{1,0:T(8,128)(2,1)}, bf16[10240,256]{1,0:T(8,128)(2,1)}) custom-call(f32[1,10240]{1,0:T(1,128)} %reshape.78.spacing_ref, f32[128,1]{1,0:T(8,128)} %copy.31.freq_ref, bf16[128,256]{1,0:T(8,128)(2,1)} %w_time_ref.3), custom_call_target="tpu_custom_call" | custom-call | flops 11000000512 | bytes 30000000 | tf_op jit(solution)/shard_map/phase_step/pallas_call | solution.py:227
  43.9 2.5 %collective-permute-start.2 = (s32[32,32]{1,0:T(8,128)S(1)}, s32[32,32]{1,0:T(8,128)S(1)}, u32[]{:S(2)}, u32[]{:S(2)}) collective-permute-start(s32[32,32]{1,0:T(8,128)S(1)} %get-tuple-element.47), channel_id=1, source_target_pairs={{0,3},{1,0},{2,1},{3,2},{4,7},{5,4},{6,5},{7,6},{8,11},{9,8},{10,9... | collective-permute-start | bytes 12296 | tf_op jit(solution)/shard_map/ppermute | solution.py:599
  46.5 0.0 collective-permute-start
  46.5 1.7 collective-permute-start.1
  48.2 0.6 shift-left_or_fusion.pair_ref
  48.8 0.1 reshape.75
  48.9 0.2 copy.29
  49.1 0.8 reshape.76.nbr_ref
  49.9 0.8 collective-permute-done
  50.7 0.4 collective-permute-done.1
  51.1 0.7 reshape.74.index_ref
  51.7 31.6 %all-to-all-done.1 = bf16[32,256,256]{2,1,0:T(8,128)(2,1)} async-done(((bf16[32,256,256]{2,1,0:T(8,128)(2,1)}), bf16[32,256,256]{2,1,0:T(8,128)(2,1)}, u32[]{:S(2)}, u32[]{:S(2)}) %all-to-all-start.1) | async-done | bytes 4194336 | tf_op jit(solution)/shard_map/all_to_all | solution.py:595
  83.3 8.5 %memory_step.1 = (bf16[1024,256]{1,0:T(8,128)(2,1)}, bf16[1024,256]{1,0:T(8,128)(2,1)}, bf16[32,4,32,256]{3,2,1,0:T(8,128)(2,1)}) custom-call(s32[1024]{0:T(1024)} %shift-left_or_fusion.pair_ref, s32[1,1024]{1,0:T(1,128)} %bitcast.41, bf16[8192,256]{1,0:T(8,128)(2,1)} %bitcast.5.rows_ref, bf16[256,768]{1,0:T(8,128)(2,1)} %w_input_ref.3, ...), custom_call_target="tpu_custom_call" | custom-call | flops 8800000000 | bytes 24000000 | tf_op jit(solution)/shard_map/memory_step/pallas_call | solution.py:171
  91.8 7.9 %all-to-all-start.2 = ((bf16[128,32,256]{2,1,0:T(8,128)(2,1)}), bf16[128,32,256]{2,1,0:T(8,128)(2,1)S(1)}, u32[]{:S(2)}, u32[]{:S(2)}) async-start(bf16[128,32,256]{2,1,0:T(8,128)(2,1)} %bitcast.30), calls=%async_computation.2 | async-start | bytes 4194304 | tf_op jit(solution)/shard_map/all_to_all | solution.py:612
  99.8 29.7 %events_step.1 = bf16[5376,128]{1,0:T(8,128)(2,1)} custom-call(s32[10240]{0:T(1024)} %reshape.76.nbr_ref, bf16[8192,256]{1,0:T(8,128)(2,1)} %bitcast.5.rows_ref, bf16[128,10240]{1,0:T(8,128)(2,1)} %get-tuple-element.32.phase_ref, bf16[10240,256]{1,0:T(8,128)(2,1)} %get-tuple-element.33.timed_ref, bf16[1024,256]{1,0:T(8,128)(2,1)} %get-tuple-element.34.mem_src_ref, ...), custom_call_target="tpu_custom_call" | custom-call | flops 44000002048 | bytes 120000000 | tf_op jit(solution)/shard_map/events_step/pallas_call | solution.py:430
  129.5 1.1 all-to-all-done.2
  130.6 31.8 %all_to_all.33 = bf16[2688,2,128]{2,1,0:T(2,128)(2,1)S(1)} all-to-all(bf16[2688,2,128]{2,1,0:T(2,128)(2,1)} %bitcast.31), channel_id=1, replica_groups=mesh['node'=32,'rep'=4] {'node','rep'}, dimensions={0} | all-to-all | bytes 2752512 | tf_op jit(solution)/shard_map/all_to_all | solution.py:577
  162.4 1.4 total_parts.1
  163.8 3.8 %all-to-all-start.4 = ((bf16[2688,2,128]{2,1,0:T(2,128)(2,1)}), bf16[2688,2,128]{2,1,0:T(2,128)(2,1)S(1)}, u32[]{:S(2)}, u32[]{:S(2)}) async-start(bf16[2688,2,128]{2,1,0:T(2,128)(2,1)} %bitcast.19), calls=%async_computation.4 | async-start | bytes 2752512 | tf_op jit(solution)/shard_map/all_to_all | solution.py:577
  167.7 11.5 %merge_rows.1 = bf16[4096,256]{1,0:T(8,128)(2,1)} custom-call(s32[1]{0:T(128)} %bitcast.place_ref, s32[4096]{0:T(1024)} %reshape.74.index_ref, bf16[4096,256]{1,0:T(8,128)(2,1)} %bitcast.29, bf16[4096,256]{1,0:T(8,128)(2,1)} %memory_ref.1), custom_call_target="tpu_custom_call" | custom-call | flops 12099999744 | bytes 33000000 | tf_op jit(solution)/shard_map/merge_rows/pallas_call | solution.py:505
  179.1 11.7 %all-to-all-done.4 = bf16[2688,2,128]{2,1,0:T(2,128)(2,1)S(1)} async-done(((bf16[2688,2,128]{2,1,0:T(2,128)(2,1)}), bf16[2688,2,128]{2,1,0:T(2,128)(2,1)S(1)}, u32[]{:S(2)}, u32[]{:S(2)}) %all-to-all-start.4) | async-done | bytes 1376288 | tf_op jit(solution)/shard_map/all_to_all | solution.py:577
  190.9 1.6 unpack_grads.1
  (19 shorter events, 0.1 us)
Async XLA Ops:
  27.9 5.1 %copy-start.2 = (s32[1024,10]{0,1:T(8,128)S(1)}, s32[1024,10]{0,1:T(8,128)}, u32[]{:S(2)}) copy-start(s32[1024,10]{0,1:T(8,128)} %param.22) | copy-start | bytes 122884
  27.9 5.1 %copy-start.4 = (s32[1024]{0:T(1024)S(1)}, s32[1024]{0:T(1024)}, u32[]{:S(2)}) copy-start(s32[1024]{0:T(1024)} %param.21) | copy-start | bytes 12292
  27.9 6.3 %copy-start.7 = (f32[128]{0:T(128)S(1)}, f32[128]{0:T(128)}, u32[]{:S(2)}) copy-start(f32[128]{0:T(128)} %param.23) | copy-start | bytes 1540
  27.9 7.0 %copy-start.3 = (s32[1024,10]{0,1:T(8,128)S(1)}, s32[1024,10]{0,1:T(8,128)}, u32[]{:S(2)}) copy-start(s32[1024,10]{0,1:T(8,128)} %param.20) | copy-start | bytes 122884
  27.9 55.4 %all-to-all-start.1 = ((bf16[32,256,256]{2,1,0:T(8,128)(2,1)}), bf16[32,256,256]{2,1,0:T(8,128)(2,1)}, u32[]{:S(2)}, u32[]{:S(2)}) async-start(bf16[32,256,256]{2,1,0:T(8,128)(2,1)} %bitcast.28), calls=%async_computation.1 | async-start | bytes 8388608 | tf_op jit(solution)/shard_map/all_to_all | solution.py:595
  34.9 9.0 %copy-start.1 = (s32[32,1,128]{2,1,0:T(1,128)S(1)}, s32[32,1,128]{2,1,0:T(1,128)}, u32[]{:S(2)}) copy-start(s32[32,1,128]{2,1,0:T(1,128)} %all_to_all.32) | copy-start | bytes 49156
  34.9 13.3 %copy-start.5 = (s32[1024]{0:T(1024)S(1)}, s32[1024]{0:T(1024)}, u32[]{:S(2)}) copy-start(s32[1024]{0:T(1024)} %param.19) | copy-start | bytes 12292
  34.9 13.3 %copy-start.6 = (s32[1024]{0:T(1024)S(1)}, s32[1024]{0:T(1024)}, u32[]{:S(2)}) copy-start(s32[1024]{0:T(1024)} %param.18) | copy-start | bytes 12292
  43.9 6.0 %collective-permute-start.2 = (s32[32,32]{1,0:T(8,128)S(1)}, s32[32,32]{1,0:T(8,128)S(1)}, u32[]{:S(2)}, u32[]{:S(2)}) collective-permute-start(s32[32,32]{1,0:T(8,128)S(1)} %get-tuple-element.47), channel_id=1, source_target_pairs={{0,3},{1,0},{2,1},{3,2},{4,7},{5,4},{6,5},{7,6},{8,11},{9,8},{10,9... | collective-permute-start | bytes 12296 | tf_op jit(solution)/shard_map/ppermute | solution.py:599
  46.5 4.2 %collective-permute-start = (s32[32,32]{1,0:T(8,128)S(1)}, s32[32,32]{1,0:T(8,128)S(1)}, u32[]{:S(2)}, u32[]{:S(2)}) collective-permute-start(s32[32,32]{1,0:T(8,128)S(1)} %get-tuple-element.47), channel_id=1, source_target_pairs={{0,1},{1,2},{2,3},{3,0},{4,5},{5,6},{6,7},{7,4},{8,9},{9,10},{10,1... | collective-permute-start | bytes 12296 | tf_op jit(solution)/shard_map/ppermute | solution.py:599
  46.5 4.6 %collective-permute-start.1 = (s32[32,32]{1,0:T(8,128)S(1)}, s32[32,32]{1,0:T(8,128)S(1)}, u32[]{:S(2)}, u32[]{:S(2)}) collective-permute-start(s32[32,32]{1,0:T(8,128)S(1)} %get-tuple-element.47), channel_id=1, source_target_pairs={{0,2},{1,3},{2,0},{3,1},{4,6},{5,7},{6,4},{7,5},{8,10},{9,11},{10,... | collective-permute-start | bytes 12296 | tf_op jit(solution)/shard_map/ppermute | solution.py:599
  91.8 38.8 %all-to-all-start.2 = ((bf16[128,32,256]{2,1,0:T(8,128)(2,1)}), bf16[128,32,256]{2,1,0:T(8,128)(2,1)S(1)}, u32[]{:S(2)}, u32[]{:S(2)}) async-start(bf16[128,32,256]{2,1,0:T(8,128)(2,1)} %bitcast.30), calls=%async_computation.2 | async-start | bytes 4194304 | tf_op jit(solution)/shard_map/all_to_all | solution.py:612
  130.6 33.2 %copy-start = (bf16[128,32,256]{2,1,0:T(8,128)(2,1)}, bf16[128,32,256]{2,1,0:T(8,128)(2,1)S(1)}, u32[]{:S(2)}) copy-start(bf16[128,32,256]{2,1,0:T(8,128)(2,1)S(1)} %all-to-all-done.2) | copy-start | bytes 6291460
  163.8 27.1 %all-to-all-start.4 = ((bf16[2688,2,128]{2,1,0:T(2,128)(2,1)}), bf16[2688,2,128]{2,1,0:T(2,128)(2,1)S(1)}, u32[]{:S(2)}, u32[]{:S(2)}) async-start(bf16[2688,2,128]{2,1,0:T(2,128)(2,1)} %bitcast.19), calls=%async_computation.4 | async-start | bytes 2752512 | tf_op jit(solution)/shard_map/all_to_all | solution.py:577
